TPU v7x, 256 devices: a whole 4x4x8 slice. The times are simulated.
256 devices in a mesh: row: 32 (over y_hi, z, core), col: 8 (over x, y_lo).
Axes of the slice: x: 4, y: 4 (y_hi: 2, y_lo: 2; y = y_hi * 2 + y_lo), z: 8, core: 2. Of those that a mesh axis runs over, the one named last changes fastest.
Arguments:
- queries: bfloat16 [3072, 7168], P('row', 'col'), may hold values from -8 to 8
- key_rows: bfloat16 [3072, 7168], P('row', 'col'), may hold values from -8 to 8
- value_rows: bfloat16 [3072, 7168], P('row', 'col'), may hold values from -6 to 6
- saved_output: bfloat16 [3072, 7168], P('row', 'col'), may hold values from -4 to 4
- grad_output: bfloat16 [3072, 7168], P('row', 'col'), may hold values from -6 to 6
- pair_bias: bfloat16 [2, 3072, 3072], P(None, 'row', 'col'), may hold values from -6 to 6
- chain_id: int32 [3072], replicated, may hold values from 0 to 7, as said below
- allowed_pairs: int32 [8, 8], replicated, may hold values from 0 to 1, as said below
Outputs:
- grad_queries: bfloat16 [3072, 7168], P('row', 'col')
- grad_keys: bfloat16 [3072, 7168], P('row', 'col')
- grad_values: bfloat16 [3072, 7168], P('row', 'col')
- grad_bias: bfloat16 [2, 3072, 3072], P(None, 'row', 'col')
Inputs may be any that keep to these rules, and one draw needn't show every extreme that they name: `chain_id`: chain numbers never fall along the tokens and each of the 8 chains holds at least one token. `allowed_pairs`: symmetric, with ones on the diagonal.
All inputs are finite; a program needn't handle non-finite values.
Results may differ from a plain program's by a relative error of at most 0.022.
Values may be sent and summed in bfloat16 or wider, within the bound.
No kernel may reach another device: no remote copies, remote signals or barrier semaphores. Data moves between devices by JAX's collectives and lax.ppermute only.
A program may use at most 128 MiB of HBM per device.

v0:
```python
import math

import jax
import jax.numpy as jnp
from jax import lax
from jax.sharding import PartitionSpec as P

H = 2
DH = 32


MASKED = -1000000000.0


def largest_block(key_count, limit):
    for block_size in range(min(key_count, limit), 0, -1):
        if key_count % block_size == 0:
            return block_size
    return 1


def over_blocks(update, state_in, sliced, key_start):
    key_count = sliced[0].shape[0]
    block_size = largest_block(key_count, 512)
    if block_size == key_count:
        return update(state_in, sliced, key_start)

    def advance(block_index, state_now):
        block_start = block_index * block_size
        pieces = tuple(
            (lax.dynamic_slice_in_dim(member, block_start, block_size, 0) for member in sliced)
        )
        return update(state_now, pieces, key_start + block_start)

    return lax.fori_loop(0, key_count // block_size, advance, state_in)


def per_device(
    queries, key_rows, value_rows, saved_output, grad_output, pair_bias, chain_id, allowed_pairs
):
    row_count = queries.shape[0]
    head_width = H * DH
    col_count = queries.shape[1] // head_width
    token_count = row_count * lax.axis_size("row")
    score_scale = 1.0 / math.sqrt(DH)
    row_index = lax.axis_index("row")
    q_four = queries.reshape(row_count, col_count, H, DH)
    g_four = grad_output.reshape(row_count, col_count, H, DH)
    labels = jnp.arange(allowed_pairs.shape[0], dtype=jnp.int32)
    allowed_float = allowed_pairs.astype(jnp.float32)
    own_chain = lax.dynamic_slice_in_dim(chain_id, row_index * row_count, row_count)
    own_onehot = (own_chain[:, None] == labels[None, :]).astype(jnp.float32)
    chain_reach = jnp.dot(own_onehot, allowed_float)
    full_bias = lax.all_gather(pair_bias, "col", axis=2, tiled=True)
    products = grad_output.astype(jnp.float32) * saved_output.astype(jnp.float32)
    row_delta = jnp.sum(products.reshape(row_count, col_count, H, DH), axis=3).transpose(1, 2, 0)

    def mask_of(key_start, key_count):
        key_chain = lax.dynamic_slice_in_dim(chain_id, key_start, key_count)
        key_onehot = (key_chain[:, None] == labels[None, :]).astype(jnp.float32)
        return jnp.dot(chain_reach, key_onehot.T) > 0.5

    def scores(key_piece, key_start, active):
        key_count = key_piece.shape[0]
        k_four = key_piece.reshape(key_count, col_count, H, DH)
        logits = (
            jnp.einsum("ichd,kchd->chik", q_four, k_four, preferred_element_type=jnp.float32)
            * score_scale
        )
        block_bias = lax.dynamic_slice_in_dim(full_bias, key_start, key_count, 2).astype(
            jnp.float32
        )
        return (jnp.where(active, logits + block_bias, MASKED), k_four)

    def add_stats(state_in, pieces, key_start):
        active = mask_of(key_start, pieces[0].shape[0])

        def accumulate(state_now):
            row_max, row_total = state_now
            logits, k_four = scores(pieces[0], key_start, active)
            new_max = jnp.maximum(row_max, jnp.max(logits, axis=3))
            new_total = row_total * jnp.exp(row_max - new_max) + jnp.sum(
                jnp.exp(logits - new_max[..., None]), axis=3
            )
            return (new_max, new_total)

        return accumulate(state_in)

    stats_init = (
        jnp.full((col_count, H, row_count), -jnp.inf, jnp.float32),
        jnp.zeros((col_count, H, row_count), jnp.float32),
    )
    row_max, row_total = over_blocks(
        add_stats, stats_init, (lax.all_gather(key_rows, "row", axis=0, tiled=True),), jnp.int32(0)
    )

    def add_grads(state_in, pieces, key_start):
        key_piece, value_piece = pieces
        key_count = key_piece.shape[0]
        active = mask_of(key_start, key_count)

        def accumulate(state_now):
            logits, k_four = scores(key_piece, key_start, active)
            v_four = value_piece.reshape(key_count, col_count, H, DH)
            weights = jnp.exp(logits - row_max[..., None]) / row_total[..., None]
            dweights = jnp.einsum(
                "ichd,kchd->chik", g_four, v_four, preferred_element_type=jnp.float32
            )
            dlogits = weights * (dweights - row_delta[..., None])
            dlogits_half = dlogits.astype(jnp.bfloat16)
            dq_sum = state_now[0] + jnp.einsum(
                "chik,kchd->ichd", dlogits_half, k_four, preferred_element_type=jnp.float32
            )
            db_all = lax.dynamic_update_slice_in_dim(
                state_now[1], jnp.sum(dlogits, axis=0), key_start, 2
            )
            weights_half = weights.astype(jnp.bfloat16)
            dk_block = (
                jnp.einsum(
                    "chik,ichd->kchd", dlogits_half, q_four, preferred_element_type=jnp.float32
                )
                * score_scale
            )
            dv_block = jnp.einsum(
                "chik,ichd->kchd", weights_half, g_four, preferred_element_type=jnp.float32
            )
            dk_all = lax.dynamic_update_slice_in_dim(
                state_now[2], dk_block.reshape(key_count, col_count * head_width), key_start, 0
            )
            dv_all = lax.dynamic_update_slice_in_dim(
                state_now[3], dv_block.reshape(key_count, col_count * head_width), key_start, 0
            )
            return (dq_sum, db_all, dk_all, dv_all)

        return accumulate(state_in)

    grad_init = (
        jnp.zeros((row_count, col_count, H, DH), jnp.float32),
        jnp.zeros((H, row_count, token_count), jnp.float32),
    )
    grad_init = grad_init + (
        jnp.zeros((token_count, col_count * head_width), jnp.float32),
        jnp.zeros((token_count, col_count * head_width), jnp.float32),
    )
    gradients = over_blocks(
        add_grads,
        grad_init,
        (
            lax.all_gather(key_rows, "row", axis=0, tiled=True),
            lax.all_gather(value_rows, "row", axis=0, tiled=True),
        ),
        jnp.int32(0),
    )
    dq_sum = gradients[0]
    db_all = gradients[1]
    dk_mine, dv_mine = (
        lax.psum_scatter(
            gradients[2].astype(jnp.bfloat16), "row", scatter_dimension=0, tiled=True
        ).astype(jnp.float32),
        lax.psum_scatter(
            gradients[3].astype(jnp.bfloat16), "row", scatter_dimension=0, tiled=True
        ).astype(jnp.float32),
    )
    db_mine = lax.psum_scatter(db_all.astype(jnp.bfloat16), "col", scatter_dimension=2, tiled=True)
    grad_q = (dq_sum * score_scale).reshape(row_count, col_count * head_width).astype(jnp.bfloat16)
    return (grad_q, dk_mine.astype(jnp.bfloat16), dv_mine.astype(jnp.bfloat16), db_mine)


def solution(mesh):
    return jax.shard_map(
        per_device,
        mesh=mesh,
        in_specs=(
            P("row", "col"),
            P("row", "col"),
            P("row", "col"),
            P("row", "col"),
            P("row", "col"),
            P(None, "row", "col"),
            P(),
            P(),
        ),
        out_specs=(P("row", "col"), P("row", "col"), P("row", "col"), P(None, "row", "col")),
        check_vma=False,
    )
```

profile of v0, /device:TPU:1, one launch (start us, length us, event | category | flops | bytes accessed | tf_op | source)
XLA Modules:
  0.0 704.5 jit_solution(9264993872216321766)
XLA Ops:
  14.6 92.0 %all-gather.4.cloned.1.call-done = bf16[3072,896]{1,0:T(8,128)(2,1)} async-done(((bf16[96,896]{1,0:T(8,128)(2,1)}), bf16[3072,896]{1,0:T(8,128)(2,1)}) %all-gather.4.cloned.1.call-update) | async-done | bytes 5505040 | tf_op jit(solution)/shard_map/all_gather | solution.py:149
  106.7 8.3 %copy.42 = bf16[3072,896]{0,1:T(8,128)(2,1)} copy(bf16[3072,896]{1,0:T(8,128)(2,1)} %all-gather.4.cloned.1.call-done) | data formatting | bytes 11010048
  115.0 27.7 %all-gather.6.cloned.1.call-done = bf16[2,96,3072]{2,1,0:T(8,128)(2,1)} async-done(((bf16[2,96,384]{2,1,0:T(8,128)(2,1)}), bf16[2,96,3072]{2,1,0:T(8,128)(2,1)}) %all-gather.6.cloned.1.call-update) | async-done | bytes 1179664 | tf_op jit(solution)/shard_map/all_gather | solution.py:54
  142.6 40.6 %while.36 = (s32[]{:T(128)}, f32[14,2,96]{2,1,0:T(2,128)S(1)}, f32[14,2,96]{2,1,0:T(2,128)S(1)}, s32[3072]{0:T(1024)}, bf16[96,8]{0,1:T(8,128)(2,1)S(1)}, /*inde...) while((s32[]{:T(128)}, f32[14,2,96]{2,1,0:T(2,128)S(1)}, ...), condition=%wide.region_3.0_spmd.clone, body=%wide.region_0.3_spmd.clone.sunk | while | flops 101418120 | bytes 15605954 | solution.py:35
  183.2 59.4 %all-gather.8.cloned.1.call-done = bf16[3072,896]{1,0:T(8,128)(2,1)} async-done(((bf16[96,896]{1,0:T(8,128)(2,1)}), bf16[3072,896]{1,0:T(8,128)(2,1)}) %all-gather.8.cloned.1.call-update) | async-done | bytes 5505040 | tf_op jit(solution)/shard_map/all_gather | solution.py:150
  243.8 2.8 broadcast.60.clone2
  246.6 2.8 broadcast.60.clone
  249.4 129.4 %while.37 = (s32[]{:T(128)}, f32[96,14,2,32]{0,3,2,1:T(8,128)}, bf16[2,96,3072]{2,1,0:T(8,128)(2,1)}, bf16[3072,896]{1,0:T(8,128)(2,1)}, bf16[3072,896]{1,0:T(8,...) while((s32[]{:T(128)}, f32[96,14,2,32]{0,3,2,1:T(8,128)}, ...), condition=%wide.region_7.8_spmd.clone, body=%wide.region_5.7_spmd.clone.sunk | while | flops 456093696 | bytes 51715416 | solution.py:35
  262.3 2.2 copy.59
  268.3 2.6 constant_dynamic-update-slice_fusion.6
  283.9 2.2 copy.59
  289.9 2.6 constant_dynamic-update-slice_fusion.6
  305.5 2.2 copy.59
  311.5 2.6 constant_dynamic-update-slice_fusion.6
  327.1 2.2 copy.59
  333.1 2.6 constant_dynamic-update-slice_fusion.6
  348.6 2.2 copy.59
  354.7 2.5 constant_dynamic-update-slice_fusion.6
  376.2 2.6 constant_dynamic-update-slice_fusion.6
  378.8 3.8 copy.47
  382.5 2.3 reshape.73
  386.9 37.9 %reduce-scatter.10.cloned.1.call-done = bf16[384,192]{1,0:T(8,128)(2,1)} async-done(((bf16[3072,192]{1,0:T(8,128)(2,1)}), bf16[384,192]{1,0:T(8,128)(2,1)}) %reduce-scatter.10.cloned.1.call-update) | async-done | bytes 147472
  426.6 134.8 %reduce-scatter.8.cloned.1.call-done = bf16[96,896]{1,0:T(8,128)(2,1)} async-done(((bf16[3072,896]{1,0:T(8,128)(2,1)}), bf16[96,896]{1,0:T(8,128)(2,1)}) %reduce-scatter.8.cloned.1.call-update) | async-done | bytes 172048 | tf_op jit(solution)/shard_map/reduce_scatter | solution.py:160
  561.4 136.3 %reduce-scatter.6.cloned.1.call-done = bf16[96,896]{1,0:T(8,128)(2,1)} async-done(((bf16[3072,896]{1,0:T(8,128)(2,1)}), bf16[96,896]{1,0:T(8,128)(2,1)}) %reduce-scatter.6.cloned.1.call-update) | async-done | bytes 172048 | tf_op jit(solution)/shard_map/reduce_scatter | solution.py:157
  (198 shorter events, 154.8 us)
Async XLA Ops:
  7.2 99.5 %all-gather.4.cloned.1.call-start = ((), (), s32[]{:S(2)}) async-start(), calls=%async_computation.3 | async-start | bytes 5677056 | tf_op jit(solution)/shard_map/all_gather | solution.py:149
  7.9 134.7 %all-gather.6.cloned.1.call-start = ((), (), s32[]{:S(2)}) async-start(), calls=%async_computation.4 | async-start | bytes 1327104 | tf_op jit(solution)/shard_map/all_gather | solution.py:54
  8.6 234.0 %all-gather.8.cloned.1.call-start = ((), (), s32[]{:S(2)}) async-start(), calls=%async_computation.5 | async-start | bytes 5677056 | tf_op jit(solution)/shard_map/all_gather | solution.py:150
  9.4 415.4 %reduce-scatter.10.cloned.1.call-start = ((), (), s32[]{:S(2)}) async-start(), calls=%async_computation.8 | async-start | bytes 1769472
  257.5 1.5 copy-start
  259.0 1.4 copy-start.1
  261.5 0.8 copy-start.2
  279.1 1.5 copy-start
  280.6 1.4 copy-start.1
  283.1 0.8 copy-start.2
  300.7 1.5 copy-start
  302.2 1.4 copy-start.1
  304.7 0.8 copy-start.2
  322.3 1.5 copy-start
  323.8 1.4 copy-start.1
  326.3 0.8 copy-start.2
  343.8 1.5 copy-start
  345.4 1.4 copy-start.1
  347.8 0.8 copy-start.2
  365.3 1.5 copy-start
  366.9 1.4 copy-start.1
  384.8 176.6 %reduce-scatter.8.cloned.1.call-start = ((), (), s32[]{:S(2)}) async-start(), calls=%async_computation.7 | async-start | bytes 5677056 | tf_op jit(solution)/shard_map/reduce_scatter | solution.py:160
  384.9 1.1 copy-start.3
  385.4 312.3 %reduce-scatter.6.cloned.1.call-start = ((), (), s32[]{:S(2)}) async-start(), calls=%async_computation.6 | async-start | bytes 5677056 | tf_op jit(solution)/shard_map/reduce_scatter | solution.py:157
  (1 other events, 0.8 us)
Sparse Core Ops, SparseCore 0:
  10.8 95.8 all-gather.3
  108.5 34.1 all-gather.5
  145.4 97.1 all-gather.7
  385.0 39.7 reduce-scatter.9
  429.5 131.9 reduce-scatter.7
  566.1 131.5 reduce-scatter.5
where the time goes:
time: 710 us; the launch traced here: 705 us
  waiting for transfers between devices  491 us (69%)
  local copies, waits for them, and re-layouts  114 us (16%)
  matrix products  60.3 us (8%)
  other arithmetic  24 us (3%)
  between operations  14.2 us (2%)
    reduce_scatter x1, waiting for transfers between devices, per_device(): lax.psum_scatter(gradients[2].astype(jnp.bfloat16), 'row', scatter_dimens...  136 us
    reduce_scatter x1, waiting for transfers between devices, per_device(): lax.psum_scatter(gradients[3].astype(jnp.bfloat16), 'row', scatter_dimens...  135 us
    all_gather x1, waiting for transfers between devices, per_device(): lax.all_gather(key_rows, 'row', axis=0, tiled=True)  92 us
    all_gather x1, waiting for transfers between devices, per_device(): lax.all_gather(value_rows, 'row', axis=0, tiled=True)  59.4 us
    unnamed x7, waiting for transfers between devices  41 us
    dynamic_slice x24, local copies, waits for them, and re-layouts, advance(): lax.dynamic_slice_in_dim(member, block_start, block_size, 0)  30.6 us
    dynamic_update_slice x12, local copies, waits for them, and re-layouts, accumulate(): lax.dynamic_update_slice_in_dim(state_now[3], dv_block.reshape(key_count,...  29 us
    all_gather x1, waiting for transfers between devices, per_device(): full_bias = lax.all_gather(pair_bias, 'col', axis=2, tiled=True)  27.7 us
  transfers between devices with their start and end apart: 6, of which 6 were waited for; matrix products, arithmetic and copies ran while one was open for 8% of the time, Pallas kernels for 0%

commit v1 on v0

v1 whole, which is shorter than its diff:
```python
import functools
import math

import jax
import jax.numpy as jnp
from jax import lax
from jax.experimental import pallas as pl
from jax.experimental.pallas import tpu as pltpu
from jax.sharding import PartitionSpec as P

H = 2
DH = 32
SCALE = 1.0 / math.sqrt(DH)
LOG2E = math.log2(math.e)
MASKED = -1000000000.0 * LOG2E
NY, NZ, NC = 2, 8, 2
NX, NL = 4, 2
HALF = 7

F32 = jnp.float32
BF = jnp.bfloat16
NT = (((1,), (1,)), ((), ()))
VMEM = pl.BlockSpec(memory_space=pltpu.VMEM)
SMEM = pl.BlockSpec(memory_space=pltpu.SMEM)
ANY = pl.BlockSpec(memory_space=pl.ANY)
PARAMS = pltpu.CompilerParams(vmem_limit_bytes=56 * 2**20)


def iota(shape, dim):
    return lax.broadcasted_iota(jnp.int32, shape, dim)


def row_move(array, dy, dz, dc):
    pairs = []
    for y in range(NY):
        for z in range(NZ):
            for c in range(NC):
                target = ((y ^ dy) * NZ + (z + dz) % NZ) * NC + (c ^ dc)
                pairs.append(((y * NZ + z) * NC + c, target))
    return lax.ppermute(array, "row", pairs)


def col_move(array, dx, dl):
    pairs = []
    for x in range(NX):
        for l in range(NL):
            pairs.append((x * NL + l, ((x + dx) % NX) * NL + (l ^ dl)))
    return lax.ppermute(array, "col", pairs)


def sign(index, half):
    even = 1 - 2 * (index % 2)
    return even if half == 0 else -even


def x_pair(array, half, way):
    pairs = []
    for x in range(NX):
        for l in range(NL):
            pairs.append((x * NL + l, ((x + way * sign(x, half)) % NX) * NL + l))
    return lax.ppermute(array, "col", pairs)


def picks(shape, dim):
    mine = iota(shape, dim)
    distance = iota(shape, 1 - dim) - 2 * mine + (mine & (DH - 1))

    def pick(owner):
        return (distance == (owner % 2) * (HALF * H * DH) + (owner // 2) * DH).astype(BF)

    return pick


def split_kernel(count, me_ref, *refs):
    ins, outs = refs[:count], refs[-4:]
    width = ins[0].shape[1]
    w = HALF * DH
    pick = picks((width, w), 1)
    for f in range(4):
        chosen = pick(me_ref[0] ^ f)
        for u in range(count):
            outs[f][:, u * w : (u + 1) * w] = jnp.dot(
                ins[u][...], chosen, preferred_element_type=F32
            ).astype(BF)


def split(pos, arrays, *after):
    rows = arrays[0].shape[0]
    return pl.pallas_call(
        functools.partial(split_kernel, len(arrays)),
        in_specs=[SMEM] + [VMEM] * len(arrays) + [ANY] * len(after),
        out_specs=[VMEM] * 4,
        out_shape=[jax.ShapeDtypeStruct((rows, len(arrays) * HALF * DH), BF)] * 4,
        compiler_params=PARAMS,
        name="split",
    )(pos, *arrays, *after)


def swap(parts):
    return [
        part if f == 0 else row_move(part, f // 2, 0, f % 2) for f, part in enumerate(parts)
    ]


def join_kernel(count, me_ref, *refs):
    parts, outs = refs[:4], refs[-count:]
    rows, width = outs[0].shape
    w = HALF * DH
    pick = picks((w, width), 0)
    sums = [jnp.zeros((rows, width), F32)] * count
    for f in range(4):
        chosen = pick(me_ref[0] ^ f)
        for u in range(count):
            sums[u] = sums[u] + jnp.dot(
                parts[f][:, u * w : (u + 1) * w], chosen, preferred_element_type=F32
            )
    for u in range(count):
        outs[u][...] = sums[u].astype(BF)


def join(pos, width, parts, count):
    rows = parts[0].shape[0]
    return pl.pallas_call(
        functools.partial(join_kernel, count),
        in_specs=[SMEM] + [VMEM] * 4,
        out_specs=[VMEM] * count,
        out_shape=[jax.ShapeDtypeStruct((rows, width), BF)] * count,
        compiler_params=PARAMS,
        name="join",
    )(pos, *parts)


def turn_in_kernel(pos_ref, *refs):
    parts, out = refs[:4], refs[-1]
    me = pos_ref[0]
    rows, width = parts[0].shape
    blocks = refs[-2]
    for f in range(4):
        blocks[me ^ f] = parts[f][...]
    del refs
    eye = (iota((width, width), 0) == iota((width, width), 1)).astype(BF)
    out[...] = lax.dot_general(
        eye, blocks[...].reshape(4 * rows, width), NT, preferred_element_type=F32
    ).astype(BF)


def turn_in(pos, parts):
    rows, width = parts[0].shape
    return pl.pallas_call(
        lambda pos_ref, *refs: turn_in_kernel(pos_ref, *refs[:4], refs[5], refs[4]),
        in_specs=[SMEM] + [VMEM] * 4,
        out_specs=VMEM,
        out_shape=jax.ShapeDtypeStruct((width, 4 * rows), BF),
        scratch_shapes=[pltpu.VMEM((4, rows, width), BF)],
        compiler_params=PARAMS,
        name="turn_in",
    )(pos, *parts)


def turn_out_kernel(pos_ref, in_ref, *refs):
    outs, blocks = refs[-5:-1], refs[-1]
    me = pos_ref[0]
    width, total = in_ref.shape
    eye = (iota((total, total), 0) == iota((total, total), 1)).astype(BF)
    turned = lax.dot_general(eye, in_ref[...], NT, preferred_element_type=F32).astype(BF)
    blocks[...] = turned.reshape(4, total // 4, width)
    for f in range(4):
        outs[f][...] = blocks[me ^ f]


def turn_out(pos, array, *after):
    width, total = array.shape
    return pl.pallas_call(
        turn_out_kernel,
        in_specs=[SMEM, VMEM] + [ANY] * len(after),
        out_specs=[VMEM] * 4,
        out_shape=[jax.ShapeDtypeStruct((total // 4, width), BF)] * 4,
        scratch_shapes=[pltpu.VMEM((4, total // 4, width), BF)],
        compiler_params=PARAMS,
        name="turn_out",
    )(pos, array, *after)


def exchange_slot(pos_ref, block, fy):
    x, l = pos_ref[3], pos_ref[4]
    d = ((block // NL - x) * sign(x, fy)) & (NX - 1)
    return d ^ (d >> 1), (block % NL) ^ l


def key_lanes(block, rows):
    y, z = block // NX, 2 * (block % NX)
    return [slice(((z + u) * 2 + y) * 2 * rows, ((z + u) * 2 + y + 1) * 2 * rows) for u in (0, 1)]


def bias_kernel(rows, keys, pos_ref, reach_ref, chain_ref, near_ref, far_ref, out_ref):
    for block in range(NX * NL):
        hot = (chain_ref[:, block * keys : (block + 1) * keys] == iota((8, keys), 0)).astype(BF)
        reach = jnp.dot(reach_ref[...], hot, preferred_element_type=F32)
        lanes = key_lanes(block, rows)
        for fy in range(NY):
            n, fl = exchange_slot(pos_ref, block, fy)
            for fc, ref in enumerate((near_ref, far_ref)):
                at = slice((2 * fy + fc) * rows, (2 * fy + fc + 1) * rows)
                value = jnp.where(reach[at] > 0.5, ref[fy, n, fl].astype(F32) * LOG2E, MASKED)
                out_ref[at, lanes[0]] = value[:, : 2 * rows]
                out_ref[at, lanes[1]] = value[:, 2 * rows :]


def attn_kernel(rows, keys, pos_ref, *refs):
    tokens = 32 * rows
    R = 4 * rows
    cols = HALF
    w = cols * DH
    qgo_refs, kv_ref, b2_ref = refs[:4], refs[4], refs[5]
    dq_out, (dkv_out, own_out, other_out), refs = refs[6:10], refs[10:13], refs[13:]
    kvt, b2, qcat, gcat, qt, gt, t_ref, acc, dq_acc, db_ref, in_sem, b2_sem, out_sem = refs
    ins = [
        pltpu.make_async_copy(kv_ref.at[n], kvt.at[:, pl.ds(n * R, R)], in_sem.at[n])
        for n in range(NZ)
    ]
    ins.append(pltpu.make_async_copy(b2_ref, b2, b2_sem))
    for copy in ins:
        copy.start()
    eye_w = (iota((w, w), 0) == iota((w, w), 1)).astype(BF)
    q, g, o = (
        jnp.concatenate(
            [qgo_refs[f][:, u * w : (u + 1) * w] for f in range(4)], axis=0
        )
        for u in range(3)
    )
    qt[...] = lax.dot_general(eye_w, q, NT, preferred_element_type=F32).astype(BF)
    gt[...] = lax.dot_general(eye_w, g, NT, preferred_element_type=F32).astype(BF)
    qs = q.astype(F32) * (SCALE * LOG2E)
    q_hi = qs.astype(BF)
    q_lo = (qs - q_hi.astype(F32)).astype(BF)
    go = g.astype(F32) * o.astype(F32)
    go_hi = go.astype(BF)
    go_lo = (go - go_hi.astype(F32)).astype(BF)
    for c in range(cols):
        d = slice(c * DH, (c + 1) * DH)
        qcat[c] = jnp.concatenate([q_hi[:, d], q_lo[:, d]], axis=1)
        gcat[c] = jnp.concatenate([g[:, d], go_hi[:, d], go_lo[:, d]], axis=1)
    db_ref[...] = jnp.zeros_like(db_ref)
    dq_acc[...] = jnp.zeros_like(dq_acc)
    for copy in ins:
        copy.wait()
    minus = jnp.full((2 * DH, tokens), -1.0, BF)
    tiles = [slice(u, u + 128) for u in range(0, tokens, 128)]

    def column(c, _):
        k_at = pl.ds(pl.multiple_of(c * DH, DH), DH)
        v_at = pl.ds(pl.multiple_of(w + c * DH, DH), DH)
        k = kvt[k_at, :]
        t = jnp.dot(qcat[c], jnp.concatenate([k, k], axis=0), preferred_element_type=F32)
        t = t + b2[...]
        t_ref[...] = t
        top = t[:, tiles[0]]
        for tile in tiles[1:]:
            top = jnp.maximum(top, t[:, tile])
        p = jnp.exp2(t_ref[...] - jnp.max(top, axis=1, keepdims=True))
        t_ref[...] = p
        total = p[:, tiles[0]]
        for tile in tiles[1:]:
            total = total + p[:, tile]
        inverse = 1.0 / jnp.sum(total, axis=1, keepdims=True)
        dp = jnp.dot(
            gcat[c], jnp.concatenate([kvt[v_at, :], minus], axis=0), preferred_element_type=F32
        )
        weights = t_ref[...] * inverse
        dl = weights * dp
        db_ref[...] += dl
        w_half, dl_half = weights.astype(BF), dl.astype(BF)
        dk = jnp.dot(qt[k_at, :], dl_half, preferred_element_type=F32) * SCALE
        acc[k_at, :] = dk.astype(BF)
        dv = jnp.dot(gt[k_at, :], w_half, preferred_element_type=F32)
        acc[v_at, :] = dv.astype(BF)
        dq = lax.dot_general(dl_half, kvt[:w, :], NT, preferred_element_type=F32)
        mine = iota((R, w), 1) // DH == c
        dq_acc[...] += jnp.where(mine, dq, 0.0)
        return 0

    lax.fori_loop(0, cols, column, 0)
    for f in range(4):
        dq_out[f][...] = (dq_acc[f * rows : (f + 1) * rows, :] * SCALE).astype(BF)
    outs = [
        pltpu.make_async_copy(acc.at[:, pl.ds(n * R, R)], dkv_out.at[n], out_sem.at[n])
        for n in range(NZ)
    ]
    for copy in outs:
        copy.start()
    for block in range(NX * NL):
        lanes = key_lanes(block, rows)
        for fy in range(NY):
            n, fl = exchange_slot(pos_ref, block, fy)
            for fc, out in enumerate((own_out, other_out)):
                at = slice((2 * fy + fc) * rows, (2 * fy + fc + 1) * rows)
                part = jnp.concatenate([db_ref[at, lanes[0]], db_ref[at, lanes[1]]], axis=1)
                out[fy, n, fl] = part.astype(out.dtype)
    for copy in outs:
        copy.wait()


def attn(pos, rows, keys, qgo, kv, b2):
    cols = HALF
    R, tokens, w = 4 * rows, 32 * rows, cols * DH
    outs = [
        *[jax.ShapeDtypeStruct((rows, w), BF)] * 4,
        jax.ShapeDtypeStruct((NZ, 2 * w, R), BF),
        jax.ShapeDtypeStruct((NY, NX, NL, rows, keys), F32),
        jax.ShapeDtypeStruct((NY, NX, NL, rows, keys), BF),
    ]
    scratch = [
        pltpu.VMEM((2 * w, tokens), BF),
        pltpu.VMEM((R, tokens), F32),
        pltpu.VMEM((cols, R, 2 * DH), BF),
        pltpu.VMEM((cols, R, 3 * DH), BF),
        pltpu.VMEM((w, R), BF),
        pltpu.VMEM((w, R), BF),
        pltpu.VMEM((R, tokens), F32),
        pltpu.VMEM((2 * w, tokens), BF),
        pltpu.VMEM((R, w), F32),
        pltpu.VMEM((R, tokens), F32),
        pltpu.SemaphoreType.DMA((NZ,)),
        pltpu.SemaphoreType.DMA,
        pltpu.SemaphoreType.DMA((NZ,)),
    ]
    ins = [*qgo, kv, b2]
    return pl.pallas_call(
        functools.partial(attn_kernel, rows, keys),
        in_specs=[SMEM] + [VMEM] * 4 + [ANY] * 2,
        out_specs=[VMEM] * 4 + [ANY] + [VMEM] * 2,
        out_shape=outs,
        scratch_shapes=scratch,
        compiler_params=PARAMS,
        cost_estimate=pl.CostEstimate(
            flops=9 * 10**9 * cols, bytes_accessed=10 * R * tokens, transcendentals=R * tokens * cols
        ),
        name="attn",
    )(pos, *ins)


def per_device(
    queries, key_rows, value_rows, saved_output, grad_output, pair_bias, chain_id, allowed_pairs
):
    rows, width = queries.shape
    keys = pair_bias.shape[2]
    row_index = lax.axis_index("row")
    col_index = lax.axis_index("col")
    y, z, c = row_index // (NZ * NC), (row_index // NC) % NZ, row_index % NC
    me = y * 2 + c
    pos = jnp.stack([me, y, z, col_index // NL, col_index % NL]).astype(jnp.int32)

    groups = [
        [(y * NZ + z) * NC + c for z in range(NZ)] for y in range(NY) for c in range(NC)
    ]
    bias_own = lax.dynamic_index_in_dim(pair_bias, y, 0, keepdims=False)
    bias_other = lax.dynamic_index_in_dim(pair_bias, 1 - y, 0, keepdims=False)
    bias_rows = (bias_own, row_move(bias_other, 1, 0, 0))

    kv_parts = swap(split(pos, (key_rows, value_rows)))
    kv = lax.all_gather(turn_in(pos, kv_parts), "row", axis_index_groups=groups)
    rest = swap(split(pos, (queries, grad_output, saved_output), kv_parts[3]))

    labels = jnp.arange(allowed_pairs.shape[0], dtype=jnp.int32)
    chains = chain_id.reshape(NY, NZ, NC, rows)
    chains = lax.dynamic_index_in_dim(chains, z, 1, keepdims=False)
    chains = jnp.stack(
        [
            lax.dynamic_slice(chains, (y ^ fy, c ^ fc, 0), (1, 1, rows)).reshape(rows)
            for fy, fc in ((0, 0), (0, 1), (1, 0), (1, 1))
        ]
    ).reshape(4 * rows)
    reach = jnp.dot(
        (chains[:, None] == labels[None, :]).astype(F32), (allowed_pairs == 1).astype(F32)
    ).astype(BF)
    bias_lanes = col_move(jnp.stack(bias_rows), 0, 1)
    bias_near = []
    for fy in range(NY):
        own = jnp.stack([bias_rows[fy], bias_lanes[fy]])
        both = jnp.stack([own, x_pair(own, fy, 1)])
        bias_near += [both, x_pair(both, fy, -1)]
    bias_near = jnp.stack([jnp.concatenate(bias_near[:2]), jnp.concatenate(bias_near[2:])])
    bias_far = row_move(bias_near, 0, 0, 1)
    b2 = pl.pallas_call(
        functools.partial(bias_kernel, rows, keys),
        in_specs=[SMEM] + [VMEM] * 4,
        out_specs=VMEM,
        out_shape=jax.ShapeDtypeStruct((4 * rows, 32 * rows), F32),
        compiler_params=PARAMS,
        name="bias",
    )(pos, reach, chain_id.reshape(1, -1), bias_near, bias_far)

    *dq, dkv, db_own, db_other = attn(pos, rows, keys, rest, kv, b2)
    summed = lax.psum_scatter(
        dkv.reshape(NZ * 2 * HALF * DH, 4 * rows),
        "row",
        scatter_dimension=0,
        axis_index_groups=groups,
        tiled=True,
    )
    (grad_q,) = join(pos, width, swap(dq), 1)

    db_sum = (db_own + row_move(db_other, 0, 0, 1).astype(F32)).astype(BF)
    total = []
    for fy in range(NY):
        part = x_pair(db_sum[fy, 2:], fy, -1).astype(F32) + db_sum[fy, :2].astype(F32)
        total.append(part[0] + x_pair(part[1].astype(BF), fy, 1).astype(F32))
    total = jnp.stack(total)
    total = total[:, 0] + col_move(total[:, 1].astype(BF), 0, 1).astype(F32)
    total = total.astype(BF)
    got = row_move(total[1], 1, 0, 0)
    grad_bias = jnp.where(
        y == 0, jnp.stack([total[0], got]), jnp.stack([got, total[0]])
    )
    back = swap(turn_out(pos, summed, grad_q, grad_bias))
    grad_k, grad_v = join(pos, width, back, 2)
    return grad_q, grad_k, grad_v, grad_bias


def solution(mesh):
    whole = P("row", "col")
    bias = P(None, "row", "col")
    return jax.shard_map(
        per_device,
        mesh=mesh,
        in_specs=(whole,) * 5 + (bias, P(), P()),
        out_specs=(whole, whole, whole, bias),
        check_vma=False,
    )
```

time: 710 us -> 177 us (0.25)
  waiting for transfers between devices: 491 us -> 42 us
  local copies, waits for them, and re-layouts: 114 us -> 5.32 us
  Pallas kernels: 0 us -> 61 us
  matrix products: 60.3 us -> 0.25 us
  starting transfers between devices: 0.23 us -> 51.6 us
  other arithmetic: 24 us -> 1.66 us
    reduce_scatter x2 -> x1, waiting for transfers between devices: 271 us -> 0.01 us  [per_device(): lax.psum_scatter(dkv.reshape(NZ * 2 * HALF * DH, 4 * rows), 'row', scatte...]
    all_gather x3 -> x1, waiting for transfers between devices: 179 us -> 0.1 us  [per_device(): kv = lax.all_gather(turn_in(pos, kv_parts), 'row', axis_index_groups=groups)]
    pallas_call x0 -> x8, Pallas kernels: none -> 61 us  [the longest x1 41.5 us: attn(): pl.pallas_call(functools.partial(attn_kernel, rows, keys), in_specs=[SMEM...]
    dot_general x49 -> x1, matrix products: 60.3 us -> 0.25 us  [per_device(): jnp.dot((chains[:, None] == labels[None, :]).astype(F32), (allowed_pairs...]
    ppermute x0 -> x26, starting transfers between devices: none -> 51.5 us  [the longest x16 38.4 us: row_move(): return lax.ppermute(array, 'row', pairs)]
    dynamic_update_slice x24 -> x0, local copies, waits for them, and re-layouts: 42.5 us -> none  [the longest x12 29 us: accumulate(): lax.dynamic_update_slice_in_dim(state_now[3], dv_block.reshape(key_count,...]
    ppermute x0 -> x26, waiting for transfers between devices: none -> 41.9 us  [the longest x8 17.6 us: x_pair(): return lax.ppermute(array, 'col', pairs)]
    unnamed x7 -> x2, waiting for transfers between devices: 41 us -> 0.03 us
  transfers between devices with their start and end apart: 6 -> 28, of which waited for: 6 -> 18; matrix products, arithmetic and copies ran while one was open for 8% -> 2% of each run, Pallas kernels for 0% -> 6%
where the time goes in v1:
time: 177 us; the launch traced here: 176 us
  Pallas kernels  61 us (34%)
  starting transfers between devices  51.6 us (29%)
  waiting for transfers between devices  42 us (24%)
  between operations  14.4 us (8%)
  local copies, waits for them, and re-layouts  5.32 us (3%)
    pallas_call x1, Pallas kernels, attn(): pl.pallas_call(functools.partial(attn_kernel, rows, keys), in_specs=[SMEM...  41.5 us
    ppermute x16, starting transfers between devices, row_move(): return lax.ppermute(array, 'row', pairs)  38.4 us
    ppermute x8, waiting for transfers between devices, x_pair(): return lax.ppermute(array, 'col', pairs)  17.6 us
    ppermute x16, waiting for transfers between devices, row_move(): return lax.ppermute(array, 'row', pairs)  17.6 us
    ppermute x8, starting transfers between devices, x_pair(): return lax.ppermute(array, 'col', pairs)  11.2 us
    ppermute x2, waiting for transfers between devices, col_move(): return lax.ppermute(array, 'col', pairs)  6.71 us
    pallas_call x2, Pallas kernels, split(): pl.pallas_call(functools.partial(split_kernel, len(arrays)), in_specs=[SM...  5.43 us
    pallas_call x1, Pallas kernels, per_device(): pl.pallas_call(functools.partial(bias_kernel, rows, keys), in_specs=[SMEM...  5.08 us
  transfers between devices with their start and end apart: 28, of which 18 were waited for; matrix products, arithmetic and copies ran while one was open for 2% of the time, Pallas kernels for 6%

profile of v1, /device:TPU:1, one launch (start us, length us, event | category | flops | bytes accessed | tf_op | source)
XLA Modules:
  0.0 176.2 jit_solution(12707043924046727923)
XLA Ops:
  7.9 2.5 %split.2 = (bf16[96,448]{1,0:T(8,128)(2,1)}, bf16[96,448]{1,0:T(8,128)(2,1)}, bf16[96,448]{1,0:T(8,128)(2,1)}, bf16[96,448]{1,0:T(8,128)(2,1)}) custom-call(s32[5]{0:T(128)} %stack.87.me_ref.pos_ref, bf16[96,896]{1,0:T(8,128)(2,1)} %refs_0_.2, bf16[96,896]{1,0:T(8,128)(2,1)} %refs_1_.2), custom_call_target="tpu_custom_call" | custom-call | tf_op jit(solution)/shard_map/split/pallas_call | solution.py:89
  10.4 4.3 %collective-permute-start = (bf16[96,448]{1,0:T(8,128)(2,1)}, bf16[96,448]{1,0:T(8,128)(2,1)S(1)}, u32[]{:S(2)}, u32[]{:S(2)}) collective-permute-start(bf16[96,448]{1,0:T(8,128)(2,1)} %get-tuple-element.25), channel_id=1, source_target_pairs={{0,136},{8,128},{16,152},{24,144},{32,168},{40,160},{48,184},{56,1... | collective-permute-start | bytes 258056 | tf_op jit(solution)/shard_map/ppermute | solution.py:40
  17.7 2.6 %collective-permute-done.5.refs_2_ = bf16[96,448]{1,0:T(8,128)(2,1)S(1)} collective-permute-done((bf16[96,448]{1,0:T(8,128)(2,1)}, bf16[96,448]{1,0:T(8,128)(2,1)S(1)}, u32[]{:S(2)}, u32[]{:S(2)}) %collective-permute-start.5) | collective-permute-done | bytes 86048 | tf_op jit(solution)/shard_map/ppermute | solution.py:40
  23.3 2.4 %collective-permute-start.6 = (bf16[96,384]{1,0:T(8,128)(2,1)S(1)}, bf16[96,384]{1,0:T(8,128)(2,1)S(1)}, u32[]{:S(2)}, u32[]{:S(2)}) collective-permute-start(bf16[96,384]{1,0:T(8,128)(2,1)S(1)} %get-tuple-element.58), channel_id=1, source_target_pairs={{0,128},{8,136},{16,144},{24,152},{32,160},{40,168},{48,176},{56,1... | collective-permute-start | bytes 221192 | tf_op jit(solution)/shard_map/ppermute | solution.py:40
  28.7 3.5 %collective-permute-done.7 = bf16[2,96,384]{2,1,0:T(8,128)(2,1)S(1)} collective-permute-done((bf16[2,96,384]{2,1,0:T(8,128)(2,1)S(1)}, bf16[2,96,384]{2,1,0:T(8,128)(2,1)S(1)}, u32[]{:S(2)}, u32[]{:S(2)}) %collective-permute-start.7) | collective-permute-done | bytes 147488 | tf_op jit(solution)/shard_map/ppermute | solution.py:48
  36.4 2.6 %collective-permute-start.9 = (bf16[2,2,96,384]{3,2,1,0:T(8,128)(2,1)S(1)}, bf16[2,2,96,384]{3,2,1,0:T(8,128)(2,1)S(1)}, u32[]{:S(2)}, u32[]{:S(2)}) collective-permute-start(bf16[2,2,96,384]{3,2,1,0:T(8,128)(2,1)S(1)} %pad_maximum_fusion.2), channel_id=1, source_target_pairs={{0,6},{1,7},{2,4},{3,5},{4,2},{5,3},{6,0},{7,1},{8,14},{9,15},{10,... | collective-permute-start | bytes 884744 | tf_op jit(solution)/shard_map/ppermute | solution.py:61
  39.2 6.0 %collective-permute-done.9 = bf16[2,2,96,384]{3,2,1,0:T(8,128)(2,1)S(1)} collective-permute-done((bf16[2,2,96,384]{3,2,1,0:T(8,128)(2,1)S(1)}, bf16[2,2,96,384]{3,2,1,0:T(8,128)(2,1)S(1)}, u32[]{:S(2)}, u32[]{:S(2)}) %collective-permute-start.9) | collective-permute-done | bytes 294944 | tf_op jit(solution)/shard_map/ppermute | solution.py:61
  45.5 7.2 %collective-permute-start.12 = (bf16[2,4,2,96,384]{4,3,2,1,0:T(8,128)(2,1)S(1)}, bf16[2,4,2,96,384]{4,3,2,1,0:T(8,128)(2,1)S(1)}, u32[]{:S(2)}, u32[]{:S(2)}) collective-permute-start(bf16[2,4,2,96,384]{4,3,2,1,0:T(8,128)(2,1)S(1)} %pad_maximum_fusion.near_ref), channel_id=1, source_target_pairs={{0,8},{8,0},{16,24},{24,16},{32,40},{40,32},{48,56},{56,48},{64,72... | collective-permute-start | bytes 3538952 | tf_op jit(solution)/shard_map/ppermute | solution.py:40
  52.9 2.9 %split.3 = (bf16[96,672]{1,0:T(8,128)(2,1)}, bf16[96,672]{1,0:T(8,128)(2,1)}, bf16[96,672]{1,0:T(8,128)(2,1)}, bf16[96,672]{1,0:T(8,128)(2,1)}) custom-call(s32[5]{0:T(128)} %stack.87.me_ref.pos_ref, bf16[96,896]{1,0:T(8,128)(2,1)} %refs_0_.3, bf16[96,896]{1,0:T(8,128)(2,1)} %refs_1_.3, bf16[96,896]{1,0:T(8,128)(2,1)} %refs_2_.1, bf16[96,448]{1,0:T(8,128)(2,1)} %copy-done.3), custom_call_target="tpu_custom_call" | custom-call | tf_op jit(solution)/shard_map/split/pallas_call | solution.py:89
  61.6 5.1 %bias.1.refs_5_ = f32[384,3072]{1,0:T(8,128)} custom-call(s32[5]{0:T(128)} %stack.87.me_ref.pos_ref, bf16[384,8]{1,0:T(8,128)(2,1)} %copy.14.reach_ref, s32[1,3072]{1,0:T(1,128)} %bitcast.84, bf16[2,4,2,96,384]{4,3,2,1,0:T(8,128)(2,1)} %copy-done, bf16[2,4,2,96,384]{4,3,2,1,0:T(8,128)(2,1)} %copy-done.2), custom_call_target="tpu_custom_call" | custom-call | tf_op jit(solution)/shard_map/bias/pallas_call | solution.py:384
  67.4 41.5 %attn.1 = (bf16[96,224]{1,0:T(8,128)(2,1)}, bf16[96,224]{1,0:T(8,128)(2,1)}, bf16[96,224]{1,0:T(8,128)(2,1)}, bf16[96,224]{1,0:T(8,128)(2,1)}, bf16[8,448,384]{2...) custom-call(s32[5]{0:T(128)} %stack.87.me_ref.pos_ref, ...), custom_call_target="tpu_custom_call" | custom-call | flops 62999998464 | bytes 11796480 | tf_op jit(solution)/shard_map/attn/pallas_call | solution.py:328
  109.0 2.6 %collective-permute-start.16 = (bf16[2,4,2,96,384]{4,3,2,1,0:T(8,128)(2,1)}, bf16[2,4,2,96,384]{4,3,2,1,0:T(8,128)(2,1)S(1)}, u32[]{:S(2)}, u32[]{:S(2)}) collective-permute-start(bf16[2,4,2,96,384]{4,3,2,1,0:T(8,128)(2,1)} %get-tuple-element.39), channel_id=1, source_target_pairs={{0,8},{8,0},{16,24},{24,16},{32,40},{40,32},{48,56},{56,48},{64,72... | collective-permute-start | bytes 3538952 | tf_op jit(solution)/shard_map/ppermute | solution.py:40
  111.6 2.7 %collective-permute-done.16 = bf16[2,4,2,96,384]{4,3,2,1,0:T(8,128)(2,1)S(1)} collective-permute-done((bf16[2,4,2,96,384]{4,3,2,1,0:T(8,128)(2,1)}, bf16[2,4,2,96,384]{4,3,2,1,0:T(8,128)(2,1)S(1)}, u32[]{:S(2)}, u32[]{:S(2)}) %collective-permute-start.16) | collective-permute-done | bytes 1179680 | tf_op jit(solution)/shard_map/ppermute | solution.py:40
  117.8 5.2 %collective-permute-done.19 = bf16[2,2,96,384]{3,2,1,0:T(8,128)(2,1)S(1)} collective-permute-done((bf16[2,2,96,384]{3,2,1,0:T(8,128)(2,1)S(1)}, bf16[2,2,96,384]{3,2,1,0:T(8,128)(2,1)S(1)}, u32[]{:S(2)}, u32[]{:S(2)}) %collective-permute-start.19) | collective-permute-done | bytes 294944 | tf_op jit(solution)/shard_map/ppermute | solution.py:61
  127.3 2.4 %collective-permute-done.18 = bf16[2,96,384]{2,1,0:T(8,128)(2,1)S(1)} collective-permute-done((bf16[2,96,384]{2,1,0:T(8,128)(2,1)S(1)}, bf16[2,96,384]{2,1,0:T(8,128)(2,1)S(1)}, u32[]{:S(2)}, u32[]{:S(2)}) %collective-permute-start.18) | collective-permute-done | bytes 147488 | tf_op jit(solution)/shard_map/ppermute | solution.py:61
  132.4 3.2 %collective-permute-done.21 = bf16[2,96,384]{2,1,0:T(8,128)(2,1)S(1)} collective-permute-done((bf16[2,96,384]{2,1,0:T(8,128)(2,1)S(1)}, bf16[2,96,384]{2,1,0:T(8,128)(2,1)S(1)}, u32[]{:S(2)}, u32[]{:S(2)}) %collective-permute-start.21) | collective-permute-done | bytes 147488 | tf_op jit(solution)/shard_map/ppermute | solution.py:48
  135.7 2.8 %collective-permute-start.22 = (bf16[96,384]{1,0:T(8,128)(2,1)S(1)}, bf16[96,384]{1,0:T(8,128)(2,1)S(1)}, u32[]{:S(2)}, u32[]{:S(2)}) collective-permute-start(bf16[96,384]{1,0:T(8,128)(2,1)S(1)} %get-tuple-element.51), channel_id=1, source_target_pairs={{0,128},{8,136},{16,144},{24,152},{32,160},{40,168},{48,176},{56,1... | collective-permute-start | bytes 221192 | tf_op jit(solution)/shard_map/ppermute | solution.py:40
  138.4 3.3 %collective-permute-start.13 = (bf16[96,224]{1,0:T(8,128)(2,1)S(1)}, bf16[96,224]{1,0:T(8,128)(2,1)S(1)}, u32[]{:S(2)}, u32[]{:S(2)}) collective-permute-start(bf16[96,224]{1,0:T(8,128)(2,1)S(1)} %copy-done.19), channel_id=1, source_target_pairs={{0,8},{8,0},{16,24},{24,16},{32,40},{40,32},{48,56},{56,48},{64,72... | collective-permute-start | bytes 129032 | tf_op jit(solution)/shard_map/ppermute | solution.py:40
  142.0 2.9 %collective-permute-start.15 = (bf16[96,224]{1,0:T(8,128)(2,1)S(1)}, bf16[96,224]{1,0:T(8,128)(2,1)S(1)}, u32[]{:S(2)}, u32[]{:S(2)}) collective-permute-start(bf16[96,224]{1,0:T(8,128)(2,1)S(1)} %copy-done.17), channel_id=1, source_target_pairs={{0,136},{8,128},{16,152},{24,144},{32,168},{40,160},{48,184},{56,1... | collective-permute-start | bytes 129032 | tf_op jit(solution)/shard_map/ppermute | solution.py:40
  153.3 4.0 %collective-permute-start.23 = (bf16[96,448]{1,0:T(8,128)(2,1)}, bf16[96,448]{1,0:T(8,128)(2,1)S(1)}, u32[]{:S(2)}, u32[]{:S(2)}) collective-permute-start(bf16[96,448]{1,0:T(8,128)(2,1)} %get-tuple-element.41), channel_id=1, source_target_pairs={{0,8},{8,0},{16,24},{24,16},{32,40},{40,32},{48,56},{56,48},{64,72... | collective-permute-start | bytes 258056 | tf_op jit(solution)/shard_map/ppermute | solution.py:40
  157.2 2.6 %collective-permute-start.24 = (bf16[96,448]{1,0:T(8,128)(2,1)}, bf16[96,448]{1,0:T(8,128)(2,1)S(1)}, u32[]{:S(2)}, u32[]{:S(2)}) collective-permute-start(bf16[96,448]{1,0:T(8,128)(2,1)} %get-tuple-element.42), channel_id=1, source_target_pairs={{0,128},{8,136},{16,144},{24,152},{32,160},{40,168},{48,176},{56,1... | collective-permute-start | bytes 258056 | tf_op jit(solution)/shard_map/ppermute | solution.py:40
  160.4 3.0 %collective-permute-done.24.refs_2_ = bf16[96,448]{1,0:T(8,128)(2,1)S(1)} collective-permute-done((bf16[96,448]{1,0:T(8,128)(2,1)}, bf16[96,448]{1,0:T(8,128)(2,1)S(1)}, u32[]{:S(2)}, u32[]{:S(2)}) %collective-permute-start.24) | collective-permute-done | bytes 86048 | tf_op jit(solution)/shard_map/ppermute | solution.py:40
  163.4 2.8 %collective-permute-done.25.refs_3_ = bf16[96,448]{1,0:T(8,128)(2,1)S(1)} collective-permute-done((bf16[96,448]{1,0:T(8,128)(2,1)}, bf16[96,448]{1,0:T(8,128)(2,1)S(1)}, u32[]{:S(2)}, u32[]{:S(2)}) %collective-permute-start.25) | collective-permute-done | bytes 86048 | tf_op jit(solution)/shard_map/ppermute | solution.py:40
  166.8 2.5 %join.3 = (bf16[96,896]{1,0:T(8,128)(2,1)}, bf16[96,896]{1,0:T(8,128)(2,1)}) custom-call(s32[5]{0:T(128)} %stack.87.me_ref.pos_ref, bf16[96,448]{1,0:T(8,128)(2,1)} %get-tuple-element.40.refs_0_, bf16[96,448]{1,0:T(8,128)(2,1)} %copy-done.7, bf16[96,448]{1,0:T(8,128)(2,1)} %copy-done.8, bf16[96,448]{1,0:T(8,128)(2,1)} %copy-done.9), custom_call_target="tpu_custom_call" | custom-call | tf_op jit(solution)/shard_map/join/pallas_call | solution.py:123
  (112 shorter events, 41.1 us)
Async XLA Ops:
  7.2 59.7 %all-gather.3.cloned.1.call-start = ((), (), s32[]{:S(2)}) async-start(), calls=%async_computation.2 | async-start | bytes 3096576 | tf_op jit(solution)/shard_map/all_gather | solution.py:361
  10.4 7.2 %collective-permute-start = (bf16[96,448]{1,0:T(8,128)(2,1)}, bf16[96,448]{1,0:T(8,128)(2,1)S(1)}, u32[]{:S(2)}, u32[]{:S(2)}) collective-permute-start(bf16[96,448]{1,0:T(8,128)(2,1)} %get-tuple-element.25), channel_id=1, source_target_pairs={{0,136},{8,128},{16,152},{24,144},{32,168},{40,160},{48,184},{56,1... | collective-permute-start | bytes 258056 | tf_op jit(solution)/shard_map/ppermute | solution.py:40
  14.7 5.6 %collective-permute-start.5 = (bf16[96,448]{1,0:T(8,128)(2,1)}, bf16[96,448]{1,0:T(8,128)(2,1)S(1)}, u32[]{:S(2)}, u32[]{:S(2)}) collective-permute-start(bf16[96,448]{1,0:T(8,128)(2,1)} %get-tuple-element.32), channel_id=1, source_target_pairs={{0,128},{8,136},{16,144},{24,152},{32,160},{40,168},{48,176},{56,1... | collective-permute-start | bytes 258056 | tf_op jit(solution)/shard_map/ppermute | solution.py:40
  23.2 127.9 %reduce-scatter.2.cloned.1.call-start = ((), (), s32[]{:S(2)}) async-start(), calls=%async_computation.1 | async-start | bytes 3096576 | tf_op jit(solution)/shard_map/reduce_scatter | solution.py:394
  23.3 4.8 %collective-permute-start.6 = (bf16[96,384]{1,0:T(8,128)(2,1)S(1)}, bf16[96,384]{1,0:T(8,128)(2,1)S(1)}, u32[]{:S(2)}, u32[]{:S(2)}) collective-permute-start(bf16[96,384]{1,0:T(8,128)(2,1)S(1)} %get-tuple-element.58), channel_id=1, source_target_pairs={{0,128},{8,136},{16,144},{24,152},{32,160},{40,168},{48,176},{56,1... | collective-permute-start | bytes 221192 | tf_op jit(solution)/shard_map/ppermute | solution.py:40
  33.7 5.4 %collective-permute-start.10 = (bf16[2,96,384]{2,1,0:T(8,128)(2,1)S(1)}, bf16[2,96,384]{2,1,0:T(8,128)(2,1)S(1)}, u32[]{:S(2)}, u32[]{:S(2)}) collective-permute-start(bf16[2,96,384]{2,1,0:T(8,128)(2,1)S(1)} %get-tuple-element.57), channel_id=1, source_target_pairs={{0,6},{1,7},{2,4},{3,5},{4,2},{5,3},{6,0},{7,1},{8,14},{9,15},{10,... | collective-permute-start | bytes 442376 | tf_op jit(solution)/shard_map/ppermute | solution.py:61
  36.4 8.8 %collective-permute-start.9 = (bf16[2,2,96,384]{3,2,1,0:T(8,128)(2,1)S(1)}, bf16[2,2,96,384]{3,2,1,0:T(8,128)(2,1)S(1)}, u32[]{:S(2)}, u32[]{:S(2)}) collective-permute-start(bf16[2,2,96,384]{3,2,1,0:T(8,128)(2,1)S(1)} %pad_maximum_fusion.2), channel_id=1, source_target_pairs={{0,6},{1,7},{2,4},{3,5},{4,2},{5,3},{6,0},{7,1},{8,14},{9,15},{10,... | collective-permute-start | bytes 884744 | tf_op jit(solution)/shard_map/ppermute | solution.py:61
  39.1 6.2 %collective-permute-start.11 = (bf16[2,2,96,384]{3,2,1,0:T(8,128)(2,1)S(1)}, bf16[2,2,96,384]{3,2,1,0:T(8,128)(2,1)S(1)}, u32[]{:S(2)}, u32[]{:S(2)}) collective-permute-start(bf16[2,2,96,384]{3,2,1,0:T(8,128)(2,1)S(1)} %pad_maximum_fusion.3), channel_id=1, source_target_pairs={{0,2},{1,3},{2,0},{3,1},{4,6},{5,7},{6,4},{7,5},{8,10},{9,11},{10,... | collective-permute-start | bytes 884744 | tf_op jit(solution)/shard_map/ppermute | solution.py:61
  45.5 15.0 %collective-permute-start.12 = (bf16[2,4,2,96,384]{4,3,2,1,0:T(8,128)(2,1)S(1)}, bf16[2,4,2,96,384]{4,3,2,1,0:T(8,128)(2,1)S(1)}, u32[]{:S(2)}, u32[]{:S(2)}) collective-permute-start(bf16[2,4,2,96,384]{4,3,2,1,0:T(8,128)(2,1)S(1)} %pad_maximum_fusion.near_ref), channel_id=1, source_target_pairs={{0,8},{8,0},{16,24},{24,16},{32,40},{40,32},{48,56},{56,48},{64,72... | collective-permute-start | bytes 3538952 | tf_op jit(solution)/shard_map/ppermute | solution.py:40
  55.9 10.8 %collective-permute-start.1 = (bf16[96,672]{1,0:T(8,128)(2,1)}, bf16[96,672]{1,0:T(8,128)(2,1)S(1)}, u32[]{:S(2)}, u32[]{:S(2)}) collective-permute-start(bf16[96,672]{1,0:T(8,128)(2,1)} %get-tuple-element.27), channel_id=1, source_target_pairs={{0,8},{8,0},{16,24},{24,16},{32,40},{40,32},{48,56},{56,48},{64,72... | collective-permute-start | bytes 387080 | tf_op jit(solution)/shard_map/ppermute | solution.py:40
  56.3 10.3 %collective-permute-start.2 = (bf16[96,672]{1,0:T(8,128)(2,1)}, bf16[96,672]{1,0:T(8,128)(2,1)S(1)}, u32[]{:S(2)}, u32[]{:S(2)}) collective-permute-start(bf16[96,672]{1,0:T(8,128)(2,1)} %get-tuple-element.28), channel_id=1, source_target_pairs={{0,128},{8,136},{16,144},{24,152},{32,160},{40,168},{48,176},{56,1... | collective-permute-start | bytes 387080 | tf_op jit(solution)/shard_map/ppermute | solution.py:40
  58.4 8.4 %collective-permute-start.3 = (bf16[96,672]{1,0:T(8,128)(2,1)}, bf16[96,672]{1,0:T(8,128)(2,1)S(1)}, u32[]{:S(2)}, u32[]{:S(2)}) collective-permute-start(bf16[96,672]{1,0:T(8,128)(2,1)} %get-tuple-element.29), channel_id=1, source_target_pairs={{0,136},{8,128},{16,152},{24,144},{32,168},{40,160},{48,184},{56,1... | collective-permute-start | bytes 387080 | tf_op jit(solution)/shard_map/ppermute | solution.py:40
  109.0 5.3 %collective-permute-start.16 = (bf16[2,4,2,96,384]{4,3,2,1,0:T(8,128)(2,1)}, bf16[2,4,2,96,384]{4,3,2,1,0:T(8,128)(2,1)S(1)}, u32[]{:S(2)}, u32[]{:S(2)}) collective-permute-start(bf16[2,4,2,96,384]{4,3,2,1,0:T(8,128)(2,1)} %get-tuple-element.39), channel_id=1, source_target_pairs={{0,8},{8,0},{16,24},{24,16},{32,40},{40,32},{48,56},{56,48},{64,72... | collective-permute-start | bytes 3538952 | tf_op jit(solution)/shard_map/ppermute | solution.py:40
  114.7 8.3 %collective-permute-start.19 = (bf16[2,2,96,384]{3,2,1,0:T(8,128)(2,1)S(1)}, bf16[2,2,96,384]{3,2,1,0:T(8,128)(2,1)S(1)}, u32[]{:S(2)}, u32[]{:S(2)}) collective-permute-start(bf16[2,2,96,384]{3,2,1,0:T(8,128)(2,1)S(1)} %get-tuple-element.48), channel_id=1, source_target_pairs={{0,2},{1,3},{2,0},{3,1},{4,6},{5,7},{6,4},{7,5},{8,10},{9,11},{10,... | collective-permute-start | bytes 884744 | tf_op jit(solution)/shard_map/ppermute | solution.py:61
  116.0 9.1 %collective-permute-start.17 = (bf16[2,2,96,384]{3,2,1,0:T(8,128)(2,1)S(1)}, bf16[2,2,96,384]{3,2,1,0:T(8,128)(2,1)S(1)}, u32[]{:S(2)}, u32[]{:S(2)}) collective-permute-start(bf16[2,2,96,384]{3,2,1,0:T(8,128)(2,1)S(1)} %get-tuple-element.49), channel_id=1, source_target_pairs={{0,6},{1,7},{2,4},{3,5},{4,2},{5,3},{6,0},{7,1},{8,14},{9,15},{10,... | collective-permute-start | bytes 884744 | tf_op jit(solution)/shard_map/ppermute | solution.py:61
  125.2 4.5 %collective-permute-start.18 = (bf16[2,96,384]{2,1,0:T(8,128)(2,1)S(1)}, bf16[2,96,384]{2,1,0:T(8,128)(2,1)S(1)}, u32[]{:S(2)}, u32[]{:S(2)}) collective-permute-start(bf16[2,96,384]{2,1,0:T(8,128)(2,1)S(1)} %fusion.9), channel_id=1, source_target_pairs={{0,2},{1,3},{2,0},{3,1},{4,6},{5,7},{6,4},{7,5},{8,10},{9,11},{10,... | collective-permute-start | bytes 442376 | tf_op jit(solution)/shard_map/ppermute | solution.py:61
  125.4 5.7 %collective-permute-start.20 = (bf16[2,96,384]{2,1,0:T(8,128)(2,1)S(1)}, bf16[2,96,384]{2,1,0:T(8,128)(2,1)S(1)}, u32[]{:S(2)}, u32[]{:S(2)}) collective-permute-start(bf16[2,96,384]{2,1,0:T(8,128)(2,1)S(1)} %fusion.10), channel_id=1, source_target_pairs={{0,6},{1,7},{2,4},{3,5},{4,2},{5,3},{6,0},{7,1},{8,14},{9,15},{10,... | collective-permute-start | bytes 442376 | tf_op jit(solution)/shard_map/ppermute | solution.py:61
  131.1 4.5 %collective-permute-start.21 = (bf16[2,96,384]{2,1,0:T(8,128)(2,1)S(1)}, bf16[2,96,384]{2,1,0:T(8,128)(2,1)S(1)}, u32[]{:S(2)}, u32[]{:S(2)}) collective-permute-start(bf16[2,96,384]{2,1,0:T(8,128)(2,1)S(1)} %fusion.11), channel_id=1, source_target_pairs={{0,1},{1,0},{2,3},{3,2},{4,5},{5,4},{6,7},{7,6},{8,9},{9,8},{10,11... | collective-permute-start | bytes 442376 | tf_op jit(solution)/shard_map/ppermute | solution.py:48
  135.7 14.8 %collective-permute-start.22 = (bf16[96,384]{1,0:T(8,128)(2,1)S(1)}, bf16[96,384]{1,0:T(8,128)(2,1)S(1)}, u32[]{:S(2)}, u32[]{:S(2)}) collective-permute-start(bf16[96,384]{1,0:T(8,128)(2,1)S(1)} %get-tuple-element.51), channel_id=1, source_target_pairs={{0,128},{8,136},{16,144},{24,152},{32,160},{40,168},{48,176},{56,1... | collective-permute-start | bytes 221192 | tf_op jit(solution)/shard_map/ppermute | solution.py:40
  138.4 6.5 %collective-permute-start.13 = (bf16[96,224]{1,0:T(8,128)(2,1)S(1)}, bf16[96,224]{1,0:T(8,128)(2,1)S(1)}, u32[]{:S(2)}, u32[]{:S(2)}) collective-permute-start(bf16[96,224]{1,0:T(8,128)(2,1)S(1)} %copy-done.19), channel_id=1, source_target_pairs={{0,8},{8,0},{16,24},{24,16},{32,40},{40,32},{48,56},{56,48},{64,72... | collective-permute-start | bytes 129032 | tf_op jit(solution)/shard_map/ppermute | solution.py:40
  142.0 5.7 %collective-permute-start.15 = (bf16[96,224]{1,0:T(8,128)(2,1)S(1)}, bf16[96,224]{1,0:T(8,128)(2,1)S(1)}, u32[]{:S(2)}, u32[]{:S(2)}) collective-permute-start(bf16[96,224]{1,0:T(8,128)(2,1)S(1)} %copy-done.17), channel_id=1, source_target_pairs={{0,136},{8,128},{16,152},{24,144},{32,168},{40,160},{48,184},{56,1... | collective-permute-start | bytes 129032 | tf_op jit(solution)/shard_map/ppermute | solution.py:40
  153.3 7.1 %collective-permute-start.23 = (bf16[96,448]{1,0:T(8,128)(2,1)}, bf16[96,448]{1,0:T(8,128)(2,1)S(1)}, u32[]{:S(2)}, u32[]{:S(2)}) collective-permute-start(bf16[96,448]{1,0:T(8,128)(2,1)} %get-tuple-element.41), channel_id=1, source_target_pairs={{0,8},{8,0},{16,24},{24,16},{32,40},{40,32},{48,56},{56,48},{64,72... | collective-permute-start | bytes 258056 | tf_op jit(solution)/shard_map/ppermute | solution.py:40
  157.2 6.1 %collective-permute-start.24 = (bf16[96,448]{1,0:T(8,128)(2,1)}, bf16[96,448]{1,0:T(8,128)(2,1)S(1)}, u32[]{:S(2)}, u32[]{:S(2)}) collective-permute-start(bf16[96,448]{1,0:T(8,128)(2,1)} %get-tuple-element.42), channel_id=1, source_target_pairs={{0,128},{8,136},{16,144},{24,152},{32,160},{40,168},{48,176},{56,1... | collective-permute-start | bytes 258056 | tf_op jit(solution)/shard_map/ppermute | solution.py:40
  159.8 6.4 %collective-permute-start.25 = (bf16[96,448]{1,0:T(8,128)(2,1)}, bf16[96,448]{1,0:T(8,128)(2,1)S(1)}, u32[]{:S(2)}, u32[]{:S(2)}) collective-permute-start(bf16[96,448]{1,0:T(8,128)(2,1)} %get-tuple-element.43), channel_id=1, source_target_pairs={{0,136},{8,128},{16,152},{24,144},{32,168},{40,160},{48,184},{56,1... | collective-permute-start | bytes 258056 | tf_op jit(solution)/shard_map/ppermute | solution.py:40
  (25 other events, 129.9 us)
Sparse Core Ops, SparseCore 0:
  23.3 43.5 all-gather.2
  109.1 41.8 reduce-scatter.1

commit v2 on v1

--- a/solution.py
+++ b/solution.py
@@ -16,6 +16,8 @@
 NY, NZ, NC = 2, 8, 2
 NX, NL = 4, 2
 HALF = 7
+BLOCK = 128
+PART = 3072
 
 F32 = jnp.float32
 BF = jnp.bfloat16
@@ -71,29 +73,31 @@
     return pick
 
 
-def split_kernel(count, me_ref, *refs):
-    ins, outs = refs[:count], refs[-4:]
+def split_kernel(count, flips, *refs):
+    ins, outs = refs[:count], refs[-len(flips) :]
+    row = lax.axis_index("row")
+    me = (row // (NZ * NC)) * 2 + row % NC
     width = ins[0].shape[1]
     w = HALF * DH
     pick = picks((width, w), 1)
-    for f in range(4):
-        chosen = pick(me_ref[0] ^ f)
+    for out, f in zip(outs, flips):
+        chosen = pick(me ^ f)
         for u in range(count):
-            outs[f][:, u * w : (u + 1) * w] = jnp.dot(
+            out[:, u * w : (u + 1) * w] = jnp.dot(
                 ins[u][...], chosen, preferred_element_type=F32
             ).astype(BF)
 
 
-def split(pos, arrays, *after):
+def split(flips, arrays, *after):
     rows = arrays[0].shape[0]
     return pl.pallas_call(
-        functools.partial(split_kernel, len(arrays)),
-        in_specs=[SMEM] + [VMEM] * len(arrays) + [ANY] * len(after),
-        out_specs=[VMEM] * 4,
-        out_shape=[jax.ShapeDtypeStruct((rows, len(arrays) * HALF * DH), BF)] * 4,
+        functools.partial(split_kernel, len(arrays), flips),
+        in_specs=[VMEM] * len(arrays) + [ANY] * len(after),
+        out_specs=[VMEM] * len(flips),
+        out_shape=[jax.ShapeDtypeStruct((rows, len(arrays) * HALF * DH), BF)] * len(flips),
         compiler_params=PARAMS,
         name="split",
-    )(pos, *arrays, *after)
+    )(*arrays, *after)
 
 
 def swap(parts):
@@ -213,7 +217,7 @@
     w = cols * DH
     qgo_refs, kv_ref, b2_ref = refs[:4], refs[4], refs[5]
     dq_out, (dkv_out, own_out, other_out), refs = refs[6:10], refs[10:13], refs[13:]
-    kvt, b2, qcat, gcat, qt, gt, t_ref, acc, dq_acc, db_ref, in_sem, b2_sem, out_sem = refs
+    kvt, b2, qcat, gcat, qt, gt, t_ref, acc, sums, dq_acc, db_ref, in_sem, b2_sem, out_sem = refs
     ins = [
         pltpu.make_async_copy(kv_ref.at[n], kvt.at[:, pl.ds(n * R, R)], in_sem.at[n])
         for n in range(NZ)
@@ -241,47 +245,93 @@
         qcat[c] = jnp.concatenate([q_hi[:, d], q_lo[:, d]], axis=1)
         gcat[c] = jnp.concatenate([g[:, d], go_hi[:, d], go_lo[:, d]], axis=1)
     db_ref[...] = jnp.zeros_like(db_ref)
-    dq_acc[...] = jnp.zeros_like(dq_acc)
     for copy in ins:
         copy.wait()
-    minus = jnp.full((2 * DH, tokens), -1.0, BF)
-    tiles = [slice(u, u + 128) for u in range(0, tokens, 128)]
-
-    def column(c, _):
-        k_at = pl.ds(pl.multiple_of(c * DH, DH), DH)
-        v_at = pl.ds(pl.multiple_of(w + c * DH, DH), DH)
-        k = kvt[k_at, :]
-        t = jnp.dot(qcat[c], jnp.concatenate([k, k], axis=0), preferred_element_type=F32)
-        t = t + b2[...]
-        t_ref[...] = t
-        top = t[:, tiles[0]]
-        for tile in tiles[1:]:
-            top = jnp.maximum(top, t[:, tile])
-        p = jnp.exp2(t_ref[...] - jnp.max(top, axis=1, keepdims=True))
-        t_ref[...] = p
-        total = p[:, tiles[0]]
-        for tile in tiles[1:]:
-            total = total + p[:, tile]
-        inverse = 1.0 / jnp.sum(total, axis=1, keepdims=True)
-        dp = jnp.dot(
-            gcat[c], jnp.concatenate([kvt[v_at, :], minus], axis=0), preferred_element_type=F32
+    minus = jnp.full((2 * DH, PART), -1.0, BF)
+    per_column = R // BLOCK
+    blocks = cols * per_column
+    parts = [slice(u, u + PART) for u in range(0, tokens, PART)]
+
+    def fold(combine, running, array):
+        for u in range(0, PART, 128):
+            running = combine(running, array[:, u : u + 128])
+        return running
+
+    def places(i):
+        c, r = i // per_column, i % per_column
+        return (
+            c,
+            pl.ds(pl.multiple_of(c * DH, DH), DH),
+            pl.ds(pl.multiple_of(w + c * DH, DH), DH),
+            pl.ds(pl.multiple_of(r * BLOCK, BLOCK), BLOCK),
+            r,
         )
-        weights = t_ref[...] * inverse
+
+    def score(i, slot, part, top):
+        c, k_at, _, at, _ = places(i)
+        k = kvt[k_at, part]
+        t = jnp.dot(qcat[c, at, :], jnp.concatenate([k, k], axis=0), preferred_element_type=F32)
+        t = t + b2[at, part]
+        t_ref[slot, :, part] = t
+        return fold(jnp.maximum, top, t)
+
+    def power(slot, part, top, total):
+        p = jnp.exp2(t_ref[slot, :, part] - top)
+        t_ref[slot, :, part] = p
+        return fold(jnp.add, total, p)
+
+    def grads(i, part, inverse, dq):
+        c, k_at, v_at, at, r = places(i)
+        v = jnp.concatenate([kvt[v_at, part], minus], axis=0)
+        dp = jnp.dot(gcat[c, at, :], v, preferred_element_type=F32)
+        weights = t_ref[i % 3, :, part] * inverse
         dl = weights * dp
-        db_ref[...] += dl
+        db_ref[at, part] += dl
         w_half, dl_half = weights.astype(BF), dl.astype(BF)
-        dk = jnp.dot(qt[k_at, :], dl_half, preferred_element_type=F32) * SCALE
-        acc[k_at, :] = dk.astype(BF)
-        dv = jnp.dot(gt[k_at, :], w_half, preferred_element_type=F32)
-        acc[v_at, :] = dv.astype(BF)
-        dq = lax.dot_general(dl_half, kvt[:w, :], NT, preferred_element_type=F32)
-        mine = iota((R, w), 1) // DH == c
-        dq_acc[...] += jnp.where(mine, dq, 0.0)
-        return 0
-
-    lax.fori_loop(0, cols, column, 0)
+        dk = jnp.dot(qt[k_at, at], dl_half, preferred_element_type=F32)
+        dv = jnp.dot(gt[k_at, at], w_half, preferred_element_type=F32)
+        dk = jnp.where(r == 0, 0.0, sums[0, :, part]) + dk
+        dv = jnp.where(r == 0, 0.0, sums[1, :, part]) + dv
+        sums[0, :, part] = dk
+        sums[1, :, part] = dv
+        acc[k_at, part] = (dk * SCALE).astype(BF)
+        acc[v_at, part] = dv.astype(BF)
+        return dq + lax.dot_general(dl_half, kvt[k_at, part], NT, preferred_element_type=F32)
+
+    lowest = jnp.full((BLOCK, 128), -3.0e38, F32)
+    zero = jnp.zeros((BLOCK, 128), F32)
+
+    def highest(top):
+        return jnp.max(top, axis=1, keepdims=True)
+
+    def inverted(total):
+        return 1.0 / jnp.sum(total, axis=1, keepdims=True)
+
+    top0, top1, total0 = lowest, lowest, zero
+    for part in parts:
+        top0 = score(0, 0, part, top0)
+    top0 = highest(top0)
+    for part in parts:
+        total0 = power(0, part, top0, total0)
+        top1 = score(1, 1, part, top1)
+
+    def step(i, carry):
+        top, inverse = carry
+        later = jnp.minimum(i + 2, blocks - 1)
+        new_top, total, dq = lowest, zero, jnp.zeros((BLOCK, DH), F32)
+        for part in parts:
+            dq = grads(i, part, inverse, dq)
+            total = power((i + 1) % 3, part, top, total)
+            new_top = score(later, (i + 2) % 3, part, new_top)
+        c, _, _, at, _ = places(i)
+        dq_acc[c, at, :] = dq
+        return highest(new_top), inverted(total)
+
+    lax.fori_loop(0, blocks, step, (highest(top1), inverted(total0)))
     for f in range(4):
-        dq_out[f][...] = (dq_acc[f * rows : (f + 1) * rows, :] * SCALE).astype(BF)
+        at = slice(f * rows, (f + 1) * rows)
+        dq = jnp.concatenate([dq_acc[c, at, :] for c in range(cols)], axis=1)
+        dq_out[f][...] = (dq * SCALE).astype(BF)
     outs = [
         pltpu.make_async_copy(acc.at[:, pl.ds(n * R, R)], dkv_out.at[n], out_sem.at[n])
         for n in range(NZ)
@@ -316,9 +366,10 @@
         pltpu.VMEM((cols, R, 3 * DH), BF),
         pltpu.VMEM((w, R), BF),
         pltpu.VMEM((w, R), BF),
-        pltpu.VMEM((R, tokens), F32),
+        pltpu.VMEM((3, BLOCK, tokens), F32),
         pltpu.VMEM((2 * w, tokens), BF),
-        pltpu.VMEM((R, w), F32),
+        pltpu.VMEM((2, DH, tokens), F32),
+        pltpu.VMEM((cols, R, DH), F32),
         pltpu.VMEM((R, tokens), F32),
         pltpu.SemaphoreType.DMA((NZ,)),
         pltpu.SemaphoreType.DMA,
@@ -357,9 +408,11 @@
     bias_other = lax.dynamic_index_in_dim(pair_bias, 1 - y, 0, keepdims=False)
     bias_rows = (bias_own, row_move(bias_other, 1, 0, 0))
 
-    kv_parts = swap(split(pos, (key_rows, value_rows)))
+    kv_far = split((2, 3), (key_rows, value_rows))
+    kv_near = split((0, 1), (key_rows, value_rows), kv_far[0])
+    kv_parts = swap([*kv_near, *kv_far])
     kv = lax.all_gather(turn_in(pos, kv_parts), "row", axis_index_groups=groups)
-    rest = swap(split(pos, (queries, grad_output, saved_output), kv_parts[3]))
+    rest = swap(split((0, 1, 2, 3), (queries, grad_output, saved_output), kv_parts[3]))
 
     labels = jnp.arange(allowed_pairs.shape[0], dtype=jnp.int32)
     chains = chain_id.reshape(NY, NZ, NC, rows)

time: 177 us -> 170 us (0.960)
  Pallas kernels: 61 us -> 57.2 us
    pallas_call x1, Pallas kernels: 41.5 us -> 35.8 us  [attn(): pl.pallas_call(functools.partial(attn_kernel, rows, keys), in_specs=[SMEM...]
    ppermute x16, waiting for transfers between devices: 17.6 us -> 15.5 us  [row_move(): return lax.ppermute(array, 'row', pairs)]
    pallas_call x2 -> x3, Pallas kernels: 5.43 us -> 7.35 us  [split(): pl.pallas_call(functools.partial(split_kernel, len(arrays), flips), in_sp...]
  transfers between devices with their start and end apart: 28 -> 28, of which waited for: 18 -> 17; matrix products, arithmetic and copies ran while one was open for 2% -> 2% of each run, Pallas kernels for 6% -> 7%
where the time goes in v2:
time: 170 us
  Pallas kernels  57.2 us (34%)
  starting transfers between devices  50.6 us (30%)
  waiting for transfers between devices  40.3 us (24%)
  between operations  14.3 us (8%)
  local copies, waits for them, and re-layouts  5.37 us (3%)
    ppermute x16, starting transfers between devices, row_move(): return lax.ppermute(array, 'row', pairs)  37.6 us
    pallas_call x1, Pallas kernels, attn(): pl.pallas_call(functools.partial(attn_kernel, rows, keys), in_specs=[SMEM...  35.8 us
    ppermute x8, waiting for transfers between devices, x_pair(): return lax.ppermute(array, 'col', pairs)  18 us
    ppermute x16, waiting for transfers between devices, row_move(): return lax.ppermute(array, 'row', pairs)  15.5 us
    ppermute x8, starting transfers between devices, x_pair(): return lax.ppermute(array, 'col', pairs)  11 us
    pallas_call x3, Pallas kernels, split(): pl.pallas_call(functools.partial(split_kernel, len(arrays), flips), in_sp...  7.35 us
    ppermute x2, waiting for transfers between devices, col_move(): return lax.ppermute(array, 'col', pairs)  6.68 us
    pallas_call x1, Pallas kernels, per_device(): pl.pallas_call(functools.partial(bias_kernel, rows, keys), in_specs=[SMEM...  5.09 us
  transfers between devices with their start and end apart: 28, of which 17 were waited for; matrix products, arithmetic and copies ran while one was open for 2% of the time, Pallas kernels for 7%

profile of v2, /device:TPU:1, one launch (start us, length us, event | category | flops | bytes accessed | tf_op | source)
XLA Modules:
  0.0 169.8 jit_solution(3116247360735120395)
XLA Ops:
  9.4 4.3 %collective-permute-start = (bf16[96,448]{1,0:T(8,128)(2,1)}, bf16[96,448]{1,0:T(8,128)(2,1)S(1)}, u32[]{:S(2)}, u32[]{:S(2)}) collective-permute-start(bf16[96,448]{1,0:T(8,128)(2,1)} %get-tuple-element.25), channel_id=1, source_target_pairs={{0,136},{8,128},{16,152},{24,144},{32,168},{40,160},{48,184},{56,1... | collective-permute-start | bytes 258056 | tf_op jit(solution)/shard_map/ppermute | solution.py:42
  20.7 2.2 %turn_in.1 = bf16[448,384]{1,0:T(8,128)(2,1)} custom-call(s32[5]{0:T(128)} %stack.87.pos_ref.me_ref, bf16[96,448]{1,0:T(8,128)(2,1)} %get-tuple-element.31.refs_0_, bf16[96,448]{1,0:T(8,128)(2,1)} %copy-done.6, bf16[96,448]{1,0:T(8,128)(2,1)} %copy-done.5, bf16[96,448]{1,0:T(8,128)(2,1)} %copy-done.3), custom_call_target="tpu_custom_call" | custom-call | tf_op jit(solution)/shard_map/turn_in/pallas_call | solution.py:153
  23.0 2.5 %collective-permute-start.6 = (bf16[96,384]{1,0:T(8,128)(2,1)S(1)}, bf16[96,384]{1,0:T(8,128)(2,1)S(1)}, u32[]{:S(2)}, u32[]{:S(2)}) collective-permute-start(bf16[96,384]{1,0:T(8,128)(2,1)S(1)} %get-tuple-element.58), channel_id=1, source_target_pairs={{0,128},{8,136},{16,144},{24,152},{32,160},{40,168},{48,176},{56,1... | collective-permute-start | bytes 221192 | tf_op jit(solution)/shard_map/ppermute | solution.py:42
  25.5 2.3 %collective-permute-done.6 = bf16[96,384]{1,0:T(8,128)(2,1)S(1)} collective-permute-done((bf16[96,384]{1,0:T(8,128)(2,1)S(1)}, bf16[96,384]{1,0:T(8,128)(2,1)S(1)}, u32[]{:S(2)}, u32[]{:S(2)}) %collective-permute-start.6) | collective-permute-done | bytes 73760 | tf_op jit(solution)/shard_map/ppermute | solution.py:42
  28.4 3.5 %collective-permute-done.7 = bf16[2,96,384]{2,1,0:T(8,128)(2,1)S(1)} collective-permute-done((bf16[2,96,384]{2,1,0:T(8,128)(2,1)S(1)}, bf16[2,96,384]{2,1,0:T(8,128)(2,1)S(1)}, u32[]{:S(2)}, u32[]{:S(2)}) %collective-permute-start.7) | collective-permute-done | bytes 147488 | tf_op jit(solution)/shard_map/ppermute | solution.py:50
  36.1 2.6 %collective-permute-start.9 = (bf16[2,2,96,384]{3,2,1,0:T(8,128)(2,1)S(1)}, bf16[2,2,96,384]{3,2,1,0:T(8,128)(2,1)S(1)}, u32[]{:S(2)}, u32[]{:S(2)}) collective-permute-start(bf16[2,2,96,384]{3,2,1,0:T(8,128)(2,1)S(1)} %pad_maximum_fusion.2), channel_id=1, source_target_pairs={{0,6},{1,7},{2,4},{3,5},{4,2},{5,3},{6,0},{7,1},{8,14},{9,15},{10,... | collective-permute-start | bytes 884744 | tf_op jit(solution)/shard_map/ppermute | solution.py:63
  38.8 6.2 %collective-permute-done.9 = bf16[2,2,96,384]{3,2,1,0:T(8,128)(2,1)S(1)} collective-permute-done((bf16[2,2,96,384]{3,2,1,0:T(8,128)(2,1)S(1)}, bf16[2,2,96,384]{3,2,1,0:T(8,128)(2,1)S(1)}, u32[]{:S(2)}, u32[]{:S(2)}) %collective-permute-start.9) | collective-permute-done | bytes 294944 | tf_op jit(solution)/shard_map/ppermute | solution.py:63
  45.4 6.4 %collective-permute-start.12 = (bf16[2,4,2,96,384]{4,3,2,1,0:T(8,128)(2,1)S(1)}, bf16[2,4,2,96,384]{4,3,2,1,0:T(8,128)(2,1)S(1)}, u32[]{:S(2)}, u32[]{:S(2)}) collective-permute-start(bf16[2,4,2,96,384]{4,3,2,1,0:T(8,128)(2,1)S(1)} %pad_maximum_fusion.near_ref), channel_id=1, source_target_pairs={{0,8},{8,0},{16,24},{24,16},{32,40},{40,32},{48,56},{56,48},{64,72... | collective-permute-start | bytes 3538952 | tf_op jit(solution)/shard_map/ppermute | solution.py:42
  52.0 2.9 %split.4 = (bf16[96,672]{1,0:T(8,128)(2,1)}, bf16[96,672]{1,0:T(8,128)(2,1)}, bf16[96,672]{1,0:T(8,128)(2,1)}, bf16[96,672]{1,0:T(8,128)(2,1)}) custom-call(bf16[96,896]{1,0:T(8,128)(2,1)} %refs_0_.4, bf16[96,896]{1,0:T(8,128)(2,1)} %refs_1_.4, bf16[96,896]{1,0:T(8,128)(2,1)} %refs_2_.1, bf16[96,448]{1,0:T(8,128)(2,1)} %copy-done.3), custom_call_target="tpu_custom_call" | custom-call | tf_op jit(solution)/shard_map/split/pallas_call | solution.py:93
  60.6 5.1 %bias.1.refs_5_ = f32[384,3072]{1,0:T(8,128)} custom-call(s32[5]{0:T(128)} %stack.87.pos_ref.me_ref, bf16[384,8]{1,0:T(8,128)(2,1)} %copy.14.reach_ref, s32[1,3072]{1,0:T(1,128)} %bitcast.84, bf16[2,4,2,96,384]{4,3,2,1,0:T(8,128)(2,1)} %copy-done, bf16[2,4,2,96,384]{4,3,2,1,0:T(8,128)(2,1)} %copy-done.2), custom_call_target="tpu_custom_call" | custom-call | tf_op jit(solution)/shard_map/bias/pallas_call | solution.py:437
  66.5 35.8 %attn.1 = (bf16[96,224]{1,0:T(8,128)(2,1)}, bf16[96,224]{1,0:T(8,128)(2,1)}, bf16[96,224]{1,0:T(8,128)(2,1)}, bf16[96,224]{1,0:T(8,128)(2,1)}, bf16[8,448,384]{2...) custom-call(s32[5]{0:T(128)} %stack.87.pos_ref.me_ref, ...), custom_call_target="tpu_custom_call" | custom-call | flops 62999998464 | bytes 11796480 | tf_op jit(solution)/shard_map/attn/pallas_call | solution.py:379
  102.4 2.6 %collective-permute-start.16 = (bf16[2,4,2,96,384]{4,3,2,1,0:T(8,128)(2,1)}, bf16[2,4,2,96,384]{4,3,2,1,0:T(8,128)(2,1)S(1)}, u32[]{:S(2)}, u32[]{:S(2)}) collective-permute-start(bf16[2,4,2,96,384]{4,3,2,1,0:T(8,128)(2,1)} %get-tuple-element.39), channel_id=1, source_target_pairs={{0,8},{8,0},{16,24},{24,16},{32,40},{40,32},{48,56},{56,48},{64,72... | collective-permute-start | bytes 3538952 | tf_op jit(solution)/shard_map/ppermute | solution.py:42
  105.0 2.7 %collective-permute-done.16 = bf16[2,4,2,96,384]{4,3,2,1,0:T(8,128)(2,1)S(1)} collective-permute-done((bf16[2,4,2,96,384]{4,3,2,1,0:T(8,128)(2,1)}, bf16[2,4,2,96,384]{4,3,2,1,0:T(8,128)(2,1)S(1)}, u32[]{:S(2)}, u32[]{:S(2)}) %collective-permute-start.16) | collective-permute-done | bytes 1179680 | tf_op jit(solution)/shard_map/ppermute | solution.py:42
  111.2 5.2 %collective-permute-done.19 = bf16[2,2,96,384]{3,2,1,0:T(8,128)(2,1)S(1)} collective-permute-done((bf16[2,2,96,384]{3,2,1,0:T(8,128)(2,1)S(1)}, bf16[2,2,96,384]{3,2,1,0:T(8,128)(2,1)S(1)}, u32[]{:S(2)}, u32[]{:S(2)}) %collective-permute-start.19) | collective-permute-done | bytes 294944 | tf_op jit(solution)/shard_map/ppermute | solution.py:63
  120.7 2.4 %collective-permute-done.18 = bf16[2,96,384]{2,1,0:T(8,128)(2,1)S(1)} collective-permute-done((bf16[2,96,384]{2,1,0:T(8,128)(2,1)S(1)}, bf16[2,96,384]{2,1,0:T(8,128)(2,1)S(1)}, u32[]{:S(2)}, u32[]{:S(2)}) %collective-permute-start.18) | collective-permute-done | bytes 147488 | tf_op jit(solution)/shard_map/ppermute | solution.py:63
  125.8 3.2 %collective-permute-done.21 = bf16[2,96,384]{2,1,0:T(8,128)(2,1)S(1)} collective-permute-done((bf16[2,96,384]{2,1,0:T(8,128)(2,1)S(1)}, bf16[2,96,384]{2,1,0:T(8,128)(2,1)S(1)}, u32[]{:S(2)}, u32[]{:S(2)}) %collective-permute-start.21) | collective-permute-done | bytes 147488 | tf_op jit(solution)/shard_map/ppermute | solution.py:50
  129.0 2.7 %collective-permute-start.22 = (bf16[96,384]{1,0:T(8,128)(2,1)S(1)}, bf16[96,384]{1,0:T(8,128)(2,1)S(1)}, u32[]{:S(2)}, u32[]{:S(2)}) collective-permute-start(bf16[96,384]{1,0:T(8,128)(2,1)S(1)} %get-tuple-element.51), channel_id=1, source_target_pairs={{0,128},{8,136},{16,144},{24,152},{32,160},{40,168},{48,176},{56,1... | collective-permute-start | bytes 221192 | tf_op jit(solution)/shard_map/ppermute | solution.py:42
  131.8 3.3 %collective-permute-start.13 = (bf16[96,224]{1,0:T(8,128)(2,1)S(1)}, bf16[96,224]{1,0:T(8,128)(2,1)S(1)}, u32[]{:S(2)}, u32[]{:S(2)}) collective-permute-start(bf16[96,224]{1,0:T(8,128)(2,1)S(1)} %copy-done.19), channel_id=1, source_target_pairs={{0,8},{8,0},{16,24},{24,16},{32,40},{40,32},{48,56},{56,48},{64,72... | collective-permute-start | bytes 129032 | tf_op jit(solution)/shard_map/ppermute | solution.py:42
  135.4 2.9 %collective-permute-start.15 = (bf16[96,224]{1,0:T(8,128)(2,1)S(1)}, bf16[96,224]{1,0:T(8,128)(2,1)S(1)}, u32[]{:S(2)}, u32[]{:S(2)}) collective-permute-start(bf16[96,224]{1,0:T(8,128)(2,1)S(1)} %copy-done.17), channel_id=1, source_target_pairs={{0,136},{8,128},{16,152},{24,144},{32,168},{40,160},{48,184},{56,1... | collective-permute-start | bytes 129032 | tf_op jit(solution)/shard_map/ppermute | solution.py:42
  146.6 4.0 %collective-permute-start.23 = (bf16[96,448]{1,0:T(8,128)(2,1)}, bf16[96,448]{1,0:T(8,128)(2,1)S(1)}, u32[]{:S(2)}, u32[]{:S(2)}) collective-permute-start(bf16[96,448]{1,0:T(8,128)(2,1)} %get-tuple-element.41), channel_id=1, source_target_pairs={{0,8},{8,0},{16,24},{24,16},{32,40},{40,32},{48,56},{56,48},{64,72... | collective-permute-start | bytes 258056 | tf_op jit(solution)/shard_map/ppermute | solution.py:42
  150.6 2.8 %collective-permute-start.24 = (bf16[96,448]{1,0:T(8,128)(2,1)}, bf16[96,448]{1,0:T(8,128)(2,1)S(1)}, u32[]{:S(2)}, u32[]{:S(2)}) collective-permute-start(bf16[96,448]{1,0:T(8,128)(2,1)} %get-tuple-element.42), channel_id=1, source_target_pairs={{0,128},{8,136},{16,144},{24,152},{32,160},{40,168},{48,176},{56,1... | collective-permute-start | bytes 258056 | tf_op jit(solution)/shard_map/ppermute | solution.py:42
  153.7 3.0 %collective-permute-done.24.refs_2_ = bf16[96,448]{1,0:T(8,128)(2,1)S(1)} collective-permute-done((bf16[96,448]{1,0:T(8,128)(2,1)}, bf16[96,448]{1,0:T(8,128)(2,1)S(1)}, u32[]{:S(2)}, u32[]{:S(2)}) %collective-permute-start.24) | collective-permute-done | bytes 86048 | tf_op jit(solution)/shard_map/ppermute | solution.py:42
  156.7 3.1 %collective-permute-done.25.refs_3_ = bf16[96,448]{1,0:T(8,128)(2,1)S(1)} collective-permute-done((bf16[96,448]{1,0:T(8,128)(2,1)}, bf16[96,448]{1,0:T(8,128)(2,1)S(1)}, u32[]{:S(2)}, u32[]{:S(2)}) %collective-permute-start.25) | collective-permute-done | bytes 86048 | tf_op jit(solution)/shard_map/ppermute | solution.py:42
  160.4 2.5 %join.3 = (bf16[96,896]{1,0:T(8,128)(2,1)}, bf16[96,896]{1,0:T(8,128)(2,1)}) custom-call(s32[5]{0:T(128)} %stack.87.pos_ref.me_ref, bf16[96,448]{1,0:T(8,128)(2,1)} %get-tuple-element.40.refs_0_, bf16[96,448]{1,0:T(8,128)(2,1)} %copy-done.7, bf16[96,448]{1,0:T(8,128)(2,1)} %copy-done.8, bf16[96,448]{1,0:T(8,128)(2,1)} %copy-done.9), custom_call_target="tpu_custom_call" | custom-call | tf_op jit(solution)/shard_map/join/pallas_call | solution.py:127
  (113 shorter events, 41.2 us)
Async XLA Ops:
  7.2 58.7 %all-gather.3.cloned.1.call-start = ((), (), s32[]{:S(2)}) async-start(), calls=%async_computation.2 | async-start | bytes 3096576 | tf_op jit(solution)/shard_map/all_gather | solution.py:414
  9.4 9.0 %collective-permute-start = (bf16[96,448]{1,0:T(8,128)(2,1)}, bf16[96,448]{1,0:T(8,128)(2,1)S(1)}, u32[]{:S(2)}, u32[]{:S(2)}) collective-permute-start(bf16[96,448]{1,0:T(8,128)(2,1)} %get-tuple-element.25), channel_id=1, source_target_pairs={{0,136},{8,128},{16,152},{24,144},{32,168},{40,160},{48,184},{56,1... | collective-permute-start | bytes 258056 | tf_op jit(solution)/shard_map/ppermute | solution.py:42
  13.7 6.2 %collective-permute-start.5 = (bf16[96,448]{1,0:T(8,128)(2,1)}, bf16[96,448]{1,0:T(8,128)(2,1)S(1)}, u32[]{:S(2)}, u32[]{:S(2)}) collective-permute-start(bf16[96,448]{1,0:T(8,128)(2,1)} %get-tuple-element.30.refs_2_), channel_id=1, source_target_pairs={{0,128},{8,136},{16,144},{24,152},{32,160},{40,168},{48,176},{56,1... | collective-permute-start | bytes 258056 | tf_op jit(solution)/shard_map/ppermute | solution.py:42
  22.9 121.6 %reduce-scatter.2.cloned.1.call-start = ((), (), s32[]{:S(2)}) async-start(), calls=%async_computation.1 | async-start | bytes 3096576 | tf_op jit(solution)/shard_map/reduce_scatter | solution.py:447
  23.0 4.8 %collective-permute-start.6 = (bf16[96,384]{1,0:T(8,128)(2,1)S(1)}, bf16[96,384]{1,0:T(8,128)(2,1)S(1)}, u32[]{:S(2)}, u32[]{:S(2)}) collective-permute-start(bf16[96,384]{1,0:T(8,128)(2,1)S(1)} %get-tuple-element.58), channel_id=1, source_target_pairs={{0,128},{8,136},{16,144},{24,152},{32,160},{40,168},{48,176},{56,1... | collective-permute-start | bytes 221192 | tf_op jit(solution)/shard_map/ppermute | solution.py:42
  33.3 5.4 %collective-permute-start.10 = (bf16[2,96,384]{2,1,0:T(8,128)(2,1)S(1)}, bf16[2,96,384]{2,1,0:T(8,128)(2,1)S(1)}, u32[]{:S(2)}, u32[]{:S(2)}) collective-permute-start(bf16[2,96,384]{2,1,0:T(8,128)(2,1)S(1)} %get-tuple-element.57), channel_id=1, source_target_pairs={{0,6},{1,7},{2,4},{3,5},{4,2},{5,3},{6,0},{7,1},{8,14},{9,15},{10,... | collective-permute-start | bytes 442376 | tf_op jit(solution)/shard_map/ppermute | solution.py:63
  36.1 8.9 %collective-permute-start.9 = (bf16[2,2,96,384]{3,2,1,0:T(8,128)(2,1)S(1)}, bf16[2,2,96,384]{3,2,1,0:T(8,128)(2,1)S(1)}, u32[]{:S(2)}, u32[]{:S(2)}) collective-permute-start(bf16[2,2,96,384]{3,2,1,0:T(8,128)(2,1)S(1)} %pad_maximum_fusion.2), channel_id=1, source_target_pairs={{0,6},{1,7},{2,4},{3,5},{4,2},{5,3},{6,0},{7,1},{8,14},{9,15},{10,... | collective-permute-start | bytes 884744 | tf_op jit(solution)/shard_map/ppermute | solution.py:63
  38.7 6.4 %collective-permute-start.11 = (bf16[2,2,96,384]{3,2,1,0:T(8,128)(2,1)S(1)}, bf16[2,2,96,384]{3,2,1,0:T(8,128)(2,1)S(1)}, u32[]{:S(2)}, u32[]{:S(2)}) collective-permute-start(bf16[2,2,96,384]{3,2,1,0:T(8,128)(2,1)S(1)} %pad_maximum_fusion.3), channel_id=1, source_target_pairs={{0,2},{1,3},{2,0},{3,1},{4,6},{5,7},{6,4},{7,5},{8,10},{9,11},{10,... | collective-permute-start | bytes 884744 | tf_op jit(solution)/shard_map/ppermute | solution.py:63
  45.4 14.2 %collective-permute-start.12 = (bf16[2,4,2,96,384]{4,3,2,1,0:T(8,128)(2,1)S(1)}, bf16[2,4,2,96,384]{4,3,2,1,0:T(8,128)(2,1)S(1)}, u32[]{:S(2)}, u32[]{:S(2)}) collective-permute-start(bf16[2,4,2,96,384]{4,3,2,1,0:T(8,128)(2,1)S(1)} %pad_maximum_fusion.near_ref), channel_id=1, source_target_pairs={{0,8},{8,0},{16,24},{24,16},{32,40},{40,32},{48,56},{56,48},{64,72... | collective-permute-start | bytes 3538952 | tf_op jit(solution)/shard_map/ppermute | solution.py:42
  54.9 10.8 %collective-permute-start.1 = (bf16[96,672]{1,0:T(8,128)(2,1)}, bf16[96,672]{1,0:T(8,128)(2,1)S(1)}, u32[]{:S(2)}, u32[]{:S(2)}) collective-permute-start(bf16[96,672]{1,0:T(8,128)(2,1)} %get-tuple-element.27), channel_id=1, source_target_pairs={{0,8},{8,0},{16,24},{24,16},{32,40},{40,32},{48,56},{56,48},{64,72... | collective-permute-start | bytes 387080 | tf_op jit(solution)/shard_map/ppermute | solution.py:42
  55.4 10.3 %collective-permute-start.2 = (bf16[96,672]{1,0:T(8,128)(2,1)}, bf16[96,672]{1,0:T(8,128)(2,1)S(1)}, u32[]{:S(2)}, u32[]{:S(2)}) collective-permute-start(bf16[96,672]{1,0:T(8,128)(2,1)} %get-tuple-element.28), channel_id=1, source_target_pairs={{0,128},{8,136},{16,144},{24,152},{32,160},{40,168},{48,176},{56,1... | collective-permute-start | bytes 387080 | tf_op jit(solution)/shard_map/ppermute | solution.py:42
  57.4 8.4 %collective-permute-start.3 = (bf16[96,672]{1,0:T(8,128)(2,1)}, bf16[96,672]{1,0:T(8,128)(2,1)S(1)}, u32[]{:S(2)}, u32[]{:S(2)}) collective-permute-start(bf16[96,672]{1,0:T(8,128)(2,1)} %get-tuple-element.29), channel_id=1, source_target_pairs={{0,136},{8,128},{16,152},{24,144},{32,168},{40,160},{48,184},{56,1... | collective-permute-start | bytes 387080 | tf_op jit(solution)/shard_map/ppermute | solution.py:42
  102.4 5.3 %collective-permute-start.16 = (bf16[2,4,2,96,384]{4,3,2,1,0:T(8,128)(2,1)}, bf16[2,4,2,96,384]{4,3,2,1,0:T(8,128)(2,1)S(1)}, u32[]{:S(2)}, u32[]{:S(2)}) collective-permute-start(bf16[2,4,2,96,384]{4,3,2,1,0:T(8,128)(2,1)} %get-tuple-element.39), channel_id=1, source_target_pairs={{0,8},{8,0},{16,24},{24,16},{32,40},{40,32},{48,56},{56,48},{64,72... | collective-permute-start | bytes 3538952 | tf_op jit(solution)/shard_map/ppermute | solution.py:42
  108.0 8.3 %collective-permute-start.19 = (bf16[2,2,96,384]{3,2,1,0:T(8,128)(2,1)S(1)}, bf16[2,2,96,384]{3,2,1,0:T(8,128)(2,1)S(1)}, u32[]{:S(2)}, u32[]{:S(2)}) collective-permute-start(bf16[2,2,96,384]{3,2,1,0:T(8,128)(2,1)S(1)} %get-tuple-element.48), channel_id=1, source_target_pairs={{0,2},{1,3},{2,0},{3,1},{4,6},{5,7},{6,4},{7,5},{8,10},{9,11},{10,... | collective-permute-start | bytes 884744 | tf_op jit(solution)/shard_map/ppermute | solution.py:63
  109.3 9.1 %collective-permute-start.17 = (bf16[2,2,96,384]{3,2,1,0:T(8,128)(2,1)S(1)}, bf16[2,2,96,384]{3,2,1,0:T(8,128)(2,1)S(1)}, u32[]{:S(2)}, u32[]{:S(2)}) collective-permute-start(bf16[2,2,96,384]{3,2,1,0:T(8,128)(2,1)S(1)} %get-tuple-element.49), channel_id=1, source_target_pairs={{0,6},{1,7},{2,4},{3,5},{4,2},{5,3},{6,0},{7,1},{8,14},{9,15},{10,... | collective-permute-start | bytes 884744 | tf_op jit(solution)/shard_map/ppermute | solution.py:63
  118.6 4.5 %collective-permute-start.18 = (bf16[2,96,384]{2,1,0:T(8,128)(2,1)S(1)}, bf16[2,96,384]{2,1,0:T(8,128)(2,1)S(1)}, u32[]{:S(2)}, u32[]{:S(2)}) collective-permute-start(bf16[2,96,384]{2,1,0:T(8,128)(2,1)S(1)} %fusion.9), channel_id=1, source_target_pairs={{0,2},{1,3},{2,0},{3,1},{4,6},{5,7},{6,4},{7,5},{8,10},{9,11},{10,... | collective-permute-start | bytes 442376 | tf_op jit(solution)/shard_map/ppermute | solution.py:63
  118.7 5.7 %collective-permute-start.20 = (bf16[2,96,384]{2,1,0:T(8,128)(2,1)S(1)}, bf16[2,96,384]{2,1,0:T(8,128)(2,1)S(1)}, u32[]{:S(2)}, u32[]{:S(2)}) collective-permute-start(bf16[2,96,384]{2,1,0:T(8,128)(2,1)S(1)} %fusion.10), channel_id=1, source_target_pairs={{0,6},{1,7},{2,4},{3,5},{4,2},{5,3},{6,0},{7,1},{8,14},{9,15},{10,... | collective-permute-start | bytes 442376 | tf_op jit(solution)/shard_map/ppermute | solution.py:63
  124.5 4.5 %collective-permute-start.21 = (bf16[2,96,384]{2,1,0:T(8,128)(2,1)S(1)}, bf16[2,96,384]{2,1,0:T(8,128)(2,1)S(1)}, u32[]{:S(2)}, u32[]{:S(2)}) collective-permute-start(bf16[2,96,384]{2,1,0:T(8,128)(2,1)S(1)} %fusion.11), channel_id=1, source_target_pairs={{0,1},{1,0},{2,3},{3,2},{4,5},{5,4},{6,7},{7,6},{8,9},{9,8},{10,11... | collective-permute-start | bytes 442376 | tf_op jit(solution)/shard_map/ppermute | solution.py:50
  129.0 14.8 %collective-permute-start.22 = (bf16[96,384]{1,0:T(8,128)(2,1)S(1)}, bf16[96,384]{1,0:T(8,128)(2,1)S(1)}, u32[]{:S(2)}, u32[]{:S(2)}) collective-permute-start(bf16[96,384]{1,0:T(8,128)(2,1)S(1)} %get-tuple-element.51), channel_id=1, source_target_pairs={{0,128},{8,136},{16,144},{24,152},{32,160},{40,168},{48,176},{56,1... | collective-permute-start | bytes 221192 | tf_op jit(solution)/shard_map/ppermute | solution.py:42
  131.8 6.5 %collective-permute-start.13 = (bf16[96,224]{1,0:T(8,128)(2,1)S(1)}, bf16[96,224]{1,0:T(8,128)(2,1)S(1)}, u32[]{:S(2)}, u32[]{:S(2)}) collective-permute-start(bf16[96,224]{1,0:T(8,128)(2,1)S(1)} %copy-done.19), channel_id=1, source_target_pairs={{0,8},{8,0},{16,24},{24,16},{32,40},{40,32},{48,56},{56,48},{64,72... | collective-permute-start | bytes 129032 | tf_op jit(solution)/shard_map/ppermute | solution.py:42
  135.4 5.7 %collective-permute-start.15 = (bf16[96,224]{1,0:T(8,128)(2,1)S(1)}, bf16[96,224]{1,0:T(8,128)(2,1)S(1)}, u32[]{:S(2)}, u32[]{:S(2)}) collective-permute-start(bf16[96,224]{1,0:T(8,128)(2,1)S(1)} %copy-done.17), channel_id=1, source_target_pairs={{0,136},{8,128},{16,152},{24,144},{32,168},{40,160},{48,184},{56,1... | collective-permute-start | bytes 129032 | tf_op jit(solution)/shard_map/ppermute | solution.py:42
  146.6 7.1 %collective-permute-start.23 = (bf16[96,448]{1,0:T(8,128)(2,1)}, bf16[96,448]{1,0:T(8,128)(2,1)S(1)}, u32[]{:S(2)}, u32[]{:S(2)}) collective-permute-start(bf16[96,448]{1,0:T(8,128)(2,1)} %get-tuple-element.41), channel_id=1, source_target_pairs={{0,8},{8,0},{16,24},{24,16},{32,40},{40,32},{48,56},{56,48},{64,72... | collective-permute-start | bytes 258056 | tf_op jit(solution)/shard_map/ppermute | solution.py:42
  150.6 6.1 %collective-permute-start.24 = (bf16[96,448]{1,0:T(8,128)(2,1)}, bf16[96,448]{1,0:T(8,128)(2,1)S(1)}, u32[]{:S(2)}, u32[]{:S(2)}) collective-permute-start(bf16[96,448]{1,0:T(8,128)(2,1)} %get-tuple-element.42), channel_id=1, source_target_pairs={{0,128},{8,136},{16,144},{24,152},{32,160},{40,168},{48,176},{56,1... | collective-permute-start | bytes 258056 | tf_op jit(solution)/shard_map/ppermute | solution.py:42
  153.4 6.4 %collective-permute-start.25 = (bf16[96,448]{1,0:T(8,128)(2,1)}, bf16[96,448]{1,0:T(8,128)(2,1)S(1)}, u32[]{:S(2)}, u32[]{:S(2)}) collective-permute-start(bf16[96,448]{1,0:T(8,128)(2,1)} %get-tuple-element.43), channel_id=1, source_target_pairs={{0,136},{8,128},{16,152},{24,144},{32,168},{40,160},{48,184},{56,1... | collective-permute-start | bytes 258056 | tf_op jit(solution)/shard_map/ppermute | solution.py:42
  (25 other events, 123.8 us)
Sparse Core Ops, SparseCore 0:
  23.0 42.8 all-gather.2
  102.5 41.8 reduce-scatter.1

commit v3 on v2

--- a/solution.py
+++ b/solution.py
@@ -25,7 +25,9 @@
 VMEM = pl.BlockSpec(memory_space=pltpu.VMEM)
 SMEM = pl.BlockSpec(memory_space=pltpu.SMEM)
 ANY = pl.BlockSpec(memory_space=pl.ANY)
-PARAMS = pltpu.CompilerParams(vmem_limit_bytes=56 * 2**20)
+HBM = pl.BlockSpec(memory_space=pltpu.HBM)
+SMALL = pltpu.CompilerParams(vmem_limit_bytes=16 * 2**20)
+LARGE = pltpu.CompilerParams(vmem_limit_bytes=34 * 2**20)
 
 
 def iota(shape, dim):
@@ -95,7 +97,7 @@
         in_specs=[VMEM] * len(arrays) + [ANY] * len(after),
         out_specs=[VMEM] * len(flips),
         out_shape=[jax.ShapeDtypeStruct((rows, len(arrays) * HALF * DH), BF)] * len(flips),
-        compiler_params=PARAMS,
+        compiler_params=SMALL,
         name="split",
     )(*arrays, *after)
 
@@ -129,7 +131,7 @@
         in_specs=[SMEM] + [VMEM] * 4,
         out_specs=[VMEM] * count,
         out_shape=[jax.ShapeDtypeStruct((rows, width), BF)] * count,
-        compiler_params=PARAMS,
+        compiler_params=SMALL,
         name="join",
     )(pos, *parts)
 
@@ -156,7 +158,7 @@
         out_specs=VMEM,
         out_shape=jax.ShapeDtypeStruct((width, 4 * rows), BF),
         scratch_shapes=[pltpu.VMEM((4, rows, width), BF)],
-        compiler_params=PARAMS,
+        compiler_params=SMALL,
         name="turn_in",
     )(pos, *parts)
 
@@ -180,7 +182,7 @@
         out_specs=[VMEM] * 4,
         out_shape=[jax.ShapeDtypeStruct((total // 4, width), BF)] * 4,
         scratch_shapes=[pltpu.VMEM((4, total // 4, width), BF)],
-        compiler_params=PARAMS,
+        compiler_params=SMALL,
         name="turn_out",
     )(pos, array, *after)
 
@@ -196,7 +198,7 @@
     return [slice(((z + u) * 2 + y) * 2 * rows, ((z + u) * 2 + y + 1) * 2 * rows) for u in (0, 1)]
 
 
-def bias_kernel(rows, keys, pos_ref, reach_ref, chain_ref, near_ref, far_ref, out_ref):
+def bias_kernel(rows, keys, pos_ref, reach_ref, chain_ref, near_ref, far_ref, _, out_ref):
     for block in range(NX * NL):
         hot = (chain_ref[:, block * keys : (block + 1) * keys] == iota((8, keys), 0)).astype(BF)
         reach = jnp.dot(reach_ref[...], hot, preferred_element_type=F32)
@@ -217,7 +219,8 @@
     w = cols * DH
     qgo_refs, kv_ref, b2_ref = refs[:4], refs[4], refs[5]
     dq_out, (dkv_out, own_out, other_out), refs = refs[6:10], refs[10:13], refs[13:]
-    kvt, b2, qcat, gcat, qt, gt, t_ref, acc, sums, dq_acc, db_ref, in_sem, b2_sem, out_sem = refs
+    kvt, b2, qcat, gcat, qt, gt, t_ref, acc, sums, dq_acc, db_ref, own, other = refs[:13]
+    in_sem, b2_sem, out_sem, db_sem = refs[13:]
     ins = [
         pltpu.make_async_copy(kv_ref.at[n], kvt.at[:, pl.ds(n * R, R)], in_sem.at[n])
         for n in range(NZ)
@@ -338,14 +341,17 @@
     ]
     for copy in outs:
         copy.start()
-    for block in range(NX * NL):
-        lanes = key_lanes(block, rows)
+    for fc, (stage, out) in enumerate(((own, own_out), (other, other_out))):
         for fy in range(NY):
-            n, fl = exchange_slot(pos_ref, block, fy)
-            for fc, out in enumerate((own_out, other_out)):
+            for block in range(NX * NL):
+                lanes = key_lanes(block, rows)
+                n, fl = exchange_slot(pos_ref, block, fy)
                 at = slice((2 * fy + fc) * rows, (2 * fy + fc + 1) * rows)
                 part = jnp.concatenate([db_ref[at, lanes[0]], db_ref[at, lanes[1]]], axis=1)
-                out[fy, n, fl] = part.astype(out.dtype)
+                stage[fy, n, fl] = part.astype(stage.dtype)
+            copy = pltpu.make_async_copy(stage.at[fy], out.at[fy], db_sem.at[2 * fc + fy])
+            copy.start()
+            outs.append(copy)
     for copy in outs:
         copy.wait()
 
@@ -371,18 +377,21 @@
         pltpu.VMEM((2, DH, tokens), F32),
         pltpu.VMEM((cols, R, DH), F32),
         pltpu.VMEM((R, tokens), F32),
+        pltpu.VMEM((NY, NX, NL, rows, keys), F32),
+        pltpu.VMEM((NY, NX, NL, rows, keys), BF),
         pltpu.SemaphoreType.DMA((NZ,)),
         pltpu.SemaphoreType.DMA,
         pltpu.SemaphoreType.DMA((NZ,)),
+        pltpu.SemaphoreType.DMA((2 * NY,)),
     ]
     ins = [*qgo, kv, b2]
     return pl.pallas_call(
         functools.partial(attn_kernel, rows, keys),
-        in_specs=[SMEM] + [VMEM] * 4 + [ANY] * 2,
-        out_specs=[VMEM] * 4 + [ANY] + [VMEM] * 2,
+        in_specs=[SMEM] + [VMEM] * 4 + [HBM, ANY],
+        out_specs=[VMEM] * 4 + [HBM] * 3,
         out_shape=outs,
         scratch_shapes=scratch,
-        compiler_params=PARAMS,
+        compiler_params=LARGE,
         cost_estimate=pl.CostEstimate(
             flops=9 * 10**9 * cols, bytes_accessed=10 * R * tokens, transcendentals=R * tokens * cols
         ),
@@ -436,12 +445,12 @@
     bias_far = row_move(bias_near, 0, 0, 1)
     b2 = pl.pallas_call(
         functools.partial(bias_kernel, rows, keys),
-        in_specs=[SMEM] + [VMEM] * 4,
+        in_specs=[SMEM] + [VMEM] * 4 + [HBM],
         out_specs=VMEM,
         out_shape=jax.ShapeDtypeStruct((4 * rows, 32 * rows), F32),
-        compiler_params=PARAMS,
+        compiler_params=SMALL,
         name="bias",
-    )(pos, reach, chain_id.reshape(1, -1), bias_near, bias_far)
+    )(pos, reach, chain_id.reshape(1, -1), bias_near, bias_far, kv)
 
     *dq, dkv, db_own, db_other = attn(pos, rows, keys, rest, kv, b2)
     summed = lax.psum_scatter(

time: 170 us -> 168 us (0.988)
  Pallas kernels: 57.2 us -> 42.7 us
  waiting for transfers between devices: 40.3 us -> 50.9 us
  local copies, waits for them, and re-layouts: 5.37 us -> 7.2 us
    all_gather x1, waiting for transfers between devices: 0.07 us -> 7.99 us  [per_device(): kv = lax.all_gather(turn_in(pos, kv_parts), 'row', axis_index_groups=groups)]
    pallas_call x3, Pallas kernels: 7.35 us -> 2.83 us  [split(): pl.pallas_call(functools.partial(split_kernel, len(arrays), flips), in_sp...]
    pallas_call x1, Pallas kernels: 35.8 us -> 31.8 us  [attn(): pl.pallas_call(functools.partial(attn_kernel, rows, keys), in_specs=[SMEM...]
    pallas_call x1, Pallas kernels: 5.09 us -> 1.71 us  [per_device(): pl.pallas_call(functools.partial(bias_kernel, rows, keys), in_specs=[SMEM...]
    unnamed x42 -> x28, local copies, waits for them, and re-layouts: 3.58 us -> 6.6 us
  transfers between devices with their start and end apart: 28 -> 28, of which waited for: 17 -> 17; matrix products, arithmetic and copies ran while one was open for 2% -> 1% of each run, Pallas kernels for 7% -> 3%
where the time goes in v3:
time: 168 us
  starting transfers between devices  51.5 us (31%)
  waiting for transfers between devices  50.9 us (30%)
  Pallas kernels  42.7 us (25%)
  between operations  14.4 us (9%)
  local copies, waits for them, and re-layouts  7.2 us (4%)
    ppermute x16, starting transfers between devices, row_move(): return lax.ppermute(array, 'row', pairs)  38.9 us
    pallas_call x1, Pallas kernels, attn(): pl.pallas_call(functools.partial(attn_kernel, rows, keys), in_specs=[SMEM...  31.8 us
    ppermute x8, waiting for transfers between devices, x_pair(): return lax.ppermute(array, 'col', pairs)  18.5 us
    ppermute x16, waiting for transfers between devices, row_move(): return lax.ppermute(array, 'row', pairs)  16.9 us
    ppermute x8, starting transfers between devices, x_pair(): return lax.ppermute(array, 'col', pairs)  10.7 us
    all_gather x1, waiting for transfers between devices, per_device(): kv = lax.all_gather(turn_in(pos, kv_parts), 'row', axis_index_groups=groups)  7.99 us
    ppermute x2, waiting for transfers between devices, col_move(): return lax.ppermute(array, 'col', pairs)  6.78 us
    unnamed x28, local copies, waits for them, and re-layouts  6.6 us
  transfers between devices with their start and end apart: 28, of which 17 were waited for; matrix products, arithmetic and copies ran while one was open for 1% of the time, Pallas kernels for 3%

profile of v3, /device:TPU:1, one launch (start us, length us, event | category | flops | bytes accessed | tf_op | source)
XLA Modules:
  0.0 168.2 jit_solution(13132646613941491231)
XLA Ops:
  9.6 4.4 %collective-permute-start = (bf16[96,448]{1,0:T(8,128)(2,1)S(1)}, bf16[96,448]{1,0:T(8,128)(2,1)S(1)}, u32[]{:S(2)}, u32[]{:S(2)}) collective-permute-start(bf16[96,448]{1,0:T(8,128)(2,1)S(1)} %get-tuple-element.25), channel_id=1, source_target_pairs={{0,136},{8,128},{16,152},{24,144},{32,168},{40,160},{48,184},{56,1... | collective-permute-start | bytes 258056 | tf_op jit(solution)/shard_map/ppermute | solution.py:44
  16.6 3.4 %collective-permute-done.5.refs_2_ = bf16[96,448]{1,0:T(8,128)(2,1)S(1)} collective-permute-done((bf16[96,448]{1,0:T(8,128)(2,1)S(1)}, bf16[96,448]{1,0:T(8,128)(2,1)S(1)}, u32[]{:S(2)}, u32[]{:S(2)}) %collective-permute-start.5) | collective-permute-done | bytes 86048 | tf_op jit(solution)/shard_map/ppermute | solution.py:44
  21.9 2.5 %collective-permute-start.6 = (bf16[96,384]{1,0:T(8,128)(2,1)S(1)}, bf16[96,384]{1,0:T(8,128)(2,1)S(1)}, u32[]{:S(2)}, u32[]{:S(2)}) collective-permute-start(bf16[96,384]{1,0:T(8,128)(2,1)S(1)} %get-tuple-element.58), channel_id=1, source_target_pairs={{0,128},{8,136},{16,144},{24,152},{32,160},{40,168},{48,176},{56,1... | collective-permute-start | bytes 221192 | tf_op jit(solution)/shard_map/ppermute | solution.py:44
  24.3 2.3 %collective-permute-done.6 = bf16[96,384]{1,0:T(8,128)(2,1)S(1)} collective-permute-done((bf16[96,384]{1,0:T(8,128)(2,1)S(1)}, bf16[96,384]{1,0:T(8,128)(2,1)S(1)}, u32[]{:S(2)}, u32[]{:S(2)}) %collective-permute-start.6) | collective-permute-done | bytes 73760 | tf_op jit(solution)/shard_map/ppermute | solution.py:44
  27.3 3.5 %collective-permute-done.7 = bf16[2,96,384]{2,1,0:T(8,128)(2,1)S(1)} collective-permute-done((bf16[2,96,384]{2,1,0:T(8,128)(2,1)S(1)}, bf16[2,96,384]{2,1,0:T(8,128)(2,1)S(1)}, u32[]{:S(2)}, u32[]{:S(2)}) %collective-permute-start.7) | collective-permute-done | bytes 147488 | tf_op jit(solution)/shard_map/ppermute | solution.py:52
  34.9 2.6 %collective-permute-start.9 = (bf16[2,2,96,384]{3,2,1,0:T(8,128)(2,1)S(1)}, bf16[2,2,96,384]{3,2,1,0:T(8,128)(2,1)S(1)}, u32[]{:S(2)}, u32[]{:S(2)}) collective-permute-start(bf16[2,2,96,384]{3,2,1,0:T(8,128)(2,1)S(1)} %pad_maximum_fusion.2), channel_id=1, source_target_pairs={{0,6},{1,7},{2,4},{3,5},{4,2},{5,3},{6,0},{7,1},{8,14},{9,15},{10,... | collective-permute-start | bytes 884744 | tf_op jit(solution)/shard_map/ppermute | solution.py:65
  37.7 6.2 %collective-permute-done.9 = bf16[2,2,96,384]{3,2,1,0:T(8,128)(2,1)S(1)} collective-permute-done((bf16[2,2,96,384]{3,2,1,0:T(8,128)(2,1)S(1)}, bf16[2,2,96,384]{3,2,1,0:T(8,128)(2,1)S(1)}, u32[]{:S(2)}, u32[]{:S(2)}) %collective-permute-start.9) | collective-permute-done | bytes 294944 | tf_op jit(solution)/shard_map/ppermute | solution.py:65
  44.2 6.4 %collective-permute-start.12 = (bf16[2,4,2,96,384]{4,3,2,1,0:T(8,128)(2,1)S(1)}, bf16[2,4,2,96,384]{4,3,2,1,0:T(8,128)(2,1)S(1)}, u32[]{:S(2)}, u32[]{:S(2)}) collective-permute-start(bf16[2,4,2,96,384]{4,3,2,1,0:T(8,128)(2,1)S(1)} %pad_maximum_fusion.near_ref), channel_id=1, source_target_pairs={{0,8},{8,0},{16,24},{24,16},{32,40},{40,32},{48,56},{56,48},{64,72... | collective-permute-start | bytes 3538952 | tf_op jit(solution)/shard_map/ppermute | solution.py:44
  53.2 2.1 %collective-permute-start.2 = (bf16[96,672]{1,0:T(8,128)(2,1)S(1)}, bf16[96,672]{1,0:T(8,128)(2,1)S(1)}, u32[]{:S(2)}, u32[]{:S(2)}) collective-permute-start(bf16[96,672]{1,0:T(8,128)(2,1)S(1)} %get-tuple-element.28), channel_id=1, source_target_pairs={{0,128},{8,136},{16,144},{24,152},{32,160},{40,168},{48,176},{56,1... | collective-permute-start | bytes 387080 | tf_op jit(solution)/shard_map/ppermute | solution.py:44
  56.8 8.0 %all-gather.3.cloned.1.call-done = bf16[3584,384]{1,0:T(8,128)(2,1)} async-done(((bf16[448,384]{1,0:T(8,128)(2,1)}), bf16[3584,384]{1,0:T(8,128)(2,1)}) %all-gather.3.cloned.1.call-update) | async-done | bytes 2752528 | tf_op jit(solution)/shard_map/all_gather | solution.py:423
  68.3 31.8 %attn.1 = (bf16[96,224]{1,0:T(8,128)(2,1)S(1)}, bf16[96,224]{1,0:T(8,128)(2,1)S(1)}, bf16[96,224]{1,0:T(8,128)(2,1)S(1)}, bf16[96,224]{1,0:T(8,128)(2,1)S(1)}, b...) custom-call(s32[5]{0:T(128)S(1)} %stack.87.pos_ref.me_ref, ...), custom_call_target="tpu_custom_call" | custom-call | flops 62999998464 | bytes 11796480 | tf_op jit(solution)/shard_map/attn/pallas_call | solution.py:388
  101.2 3.2 %collective-permute-start.16 = (bf16[2,4,2,96,384]{4,3,2,1,0:T(8,128)(2,1)}, bf16[2,4,2,96,384]{4,3,2,1,0:T(8,128)(2,1)S(1)}, u32[]{:S(2)}, u32[]{:S(2)}) collective-permute-start(bf16[2,4,2,96,384]{4,3,2,1,0:T(8,128)(2,1)} %copy-done.11), channel_id=1, source_target_pairs={{0,8},{8,0},{16,24},{24,16},{32,40},{40,32},{48,56},{56,48},{64,72... | collective-permute-start | bytes 3538952 | tf_op jit(solution)/shard_map/ppermute | solution.py:44
  104.4 2.7 %collective-permute-done.16 = bf16[2,4,2,96,384]{4,3,2,1,0:T(8,128)(2,1)S(1)} collective-permute-done((bf16[2,4,2,96,384]{4,3,2,1,0:T(8,128)(2,1)}, bf16[2,4,2,96,384]{4,3,2,1,0:T(8,128)(2,1)S(1)}, u32[]{:S(2)}, u32[]{:S(2)}) %collective-permute-start.16) | collective-permute-done | bytes 1179680 | tf_op jit(solution)/shard_map/ppermute | solution.py:44
  110.6 5.2 %collective-permute-done.19 = bf16[2,2,96,384]{3,2,1,0:T(8,128)(2,1)S(1)} collective-permute-done((bf16[2,2,96,384]{3,2,1,0:T(8,128)(2,1)S(1)}, bf16[2,2,96,384]{3,2,1,0:T(8,128)(2,1)S(1)}, u32[]{:S(2)}, u32[]{:S(2)}) %collective-permute-start.19) | collective-permute-done | bytes 294944 | tf_op jit(solution)/shard_map/ppermute | solution.py:65
  115.8 2.3 %collective-permute-done.17 = bf16[2,2,96,384]{3,2,1,0:T(8,128)(2,1)S(1)} collective-permute-done((bf16[2,2,96,384]{3,2,1,0:T(8,128)(2,1)S(1)}, bf16[2,2,96,384]{3,2,1,0:T(8,128)(2,1)S(1)}, u32[]{:S(2)}, u32[]{:S(2)}) %collective-permute-start.17) | collective-permute-done | bytes 294944 | tf_op jit(solution)/shard_map/ppermute | solution.py:65
  120.1 2.7 %collective-permute-done.18 = bf16[2,96,384]{2,1,0:T(8,128)(2,1)S(1)} collective-permute-done((bf16[2,96,384]{2,1,0:T(8,128)(2,1)S(1)}, bf16[2,96,384]{2,1,0:T(8,128)(2,1)S(1)}, u32[]{:S(2)}, u32[]{:S(2)}) %collective-permute-start.18) | collective-permute-done | bytes 147488 | tf_op jit(solution)/shard_map/ppermute | solution.py:65
  125.3 3.3 %collective-permute-done.21 = bf16[2,96,384]{2,1,0:T(8,128)(2,1)S(1)} collective-permute-done((bf16[2,96,384]{2,1,0:T(8,128)(2,1)S(1)}, bf16[2,96,384]{2,1,0:T(8,128)(2,1)S(1)}, u32[]{:S(2)}, u32[]{:S(2)}) %collective-permute-start.21) | collective-permute-done | bytes 147488 | tf_op jit(solution)/shard_map/ppermute | solution.py:52
  128.7 2.7 %collective-permute-start.22 = (bf16[96,384]{1,0:T(8,128)(2,1)S(1)}, bf16[96,384]{1,0:T(8,128)(2,1)S(1)}, u32[]{:S(2)}, u32[]{:S(2)}) collective-permute-start(bf16[96,384]{1,0:T(8,128)(2,1)S(1)} %get-tuple-element.51), channel_id=1, source_target_pairs={{0,128},{8,136},{16,144},{24,152},{32,160},{40,168},{48,176},{56,1... | collective-permute-start | bytes 221192 | tf_op jit(solution)/shard_map/ppermute | solution.py:44
  131.4 3.2 %collective-permute-start.13 = (bf16[96,224]{1,0:T(8,128)(2,1)S(1)}, bf16[96,224]{1,0:T(8,128)(2,1)S(1)}, u32[]{:S(2)}, u32[]{:S(2)}) collective-permute-start(bf16[96,224]{1,0:T(8,128)(2,1)S(1)} %get-tuple-element.34), channel_id=1, source_target_pairs={{0,8},{8,0},{16,24},{24,16},{32,40},{40,32},{48,56},{56,48},{64,72... | collective-permute-start | bytes 129032 | tf_op jit(solution)/shard_map/ppermute | solution.py:44
  134.9 2.8 %collective-permute-start.15 = (bf16[96,224]{1,0:T(8,128)(2,1)S(1)}, bf16[96,224]{1,0:T(8,128)(2,1)S(1)}, u32[]{:S(2)}, u32[]{:S(2)}) collective-permute-start(bf16[96,224]{1,0:T(8,128)(2,1)S(1)} %get-tuple-element.36), channel_id=1, source_target_pairs={{0,136},{8,128},{16,152},{24,144},{32,168},{40,160},{48,184},{56,1... | collective-permute-start | bytes 129032 | tf_op jit(solution)/shard_map/ppermute | solution.py:44
  145.9 4.5 %collective-permute-start.23 = (bf16[96,448]{1,0:T(8,128)(2,1)S(1)}, bf16[96,448]{1,0:T(8,128)(2,1)S(1)}, u32[]{:S(2)}, u32[]{:S(2)}) collective-permute-start(bf16[96,448]{1,0:T(8,128)(2,1)S(1)} %get-tuple-element.41), channel_id=1, source_target_pairs={{0,8},{8,0},{16,24},{24,16},{32,40},{40,32},{48,56},{56,48},{64,72... | collective-permute-start | bytes 258056 | tf_op jit(solution)/shard_map/ppermute | solution.py:44
  150.5 2.6 %collective-permute-start.24 = (bf16[96,448]{1,0:T(8,128)(2,1)S(1)}, bf16[96,448]{1,0:T(8,128)(2,1)S(1)}, u32[]{:S(2)}, u32[]{:S(2)}) collective-permute-start(bf16[96,448]{1,0:T(8,128)(2,1)S(1)} %get-tuple-element.42), channel_id=1, source_target_pairs={{0,128},{8,136},{16,144},{24,152},{32,160},{40,168},{48,176},{56,1... | collective-permute-start | bytes 258056 | tf_op jit(solution)/shard_map/ppermute | solution.py:44
  153.7 2.6 %collective-permute-done.24.refs_2_ = bf16[96,448]{1,0:T(8,128)(2,1)S(1)} collective-permute-done((bf16[96,448]{1,0:T(8,128)(2,1)S(1)}, bf16[96,448]{1,0:T(8,128)(2,1)S(1)}, u32[]{:S(2)}, u32[]{:S(2)}) %collective-permute-start.24) | collective-permute-done | bytes 86048 | tf_op jit(solution)/shard_map/ppermute | solution.py:44
  156.3 3.0 %collective-permute-done.25.refs_3_ = bf16[96,448]{1,0:T(8,128)(2,1)S(1)} collective-permute-done((bf16[96,448]{1,0:T(8,128)(2,1)S(1)}, bf16[96,448]{1,0:T(8,128)(2,1)S(1)}, u32[]{:S(2)}, u32[]{:S(2)}) %collective-permute-start.25) | collective-permute-done | bytes 86048 | tf_op jit(solution)/shard_map/ppermute | solution.py:44
  (99 shorter events, 39.8 us)
Async XLA Ops:
  7.2 57.6 %all-gather.3.cloned.1.call-start = ((), (), s32[]{:S(2)}) async-start(), calls=%async_computation.2 | async-start | bytes 3096576 | tf_op jit(solution)/shard_map/all_gather | solution.py:423
  9.6 7.0 %collective-permute-start = (bf16[96,448]{1,0:T(8,128)(2,1)S(1)}, bf16[96,448]{1,0:T(8,128)(2,1)S(1)}, u32[]{:S(2)}, u32[]{:S(2)}) collective-permute-start(bf16[96,448]{1,0:T(8,128)(2,1)S(1)} %get-tuple-element.25), channel_id=1, source_target_pairs={{0,136},{8,128},{16,152},{24,144},{32,168},{40,160},{48,184},{56,1... | collective-permute-start | bytes 258056 | tf_op jit(solution)/shard_map/ppermute | solution.py:44
  14.0 6.0 %collective-permute-start.5 = (bf16[96,448]{1,0:T(8,128)(2,1)S(1)}, bf16[96,448]{1,0:T(8,128)(2,1)S(1)}, u32[]{:S(2)}, u32[]{:S(2)}) collective-permute-start(bf16[96,448]{1,0:T(8,128)(2,1)S(1)} %get-tuple-element.30.refs_2_), channel_id=1, source_target_pairs={{0,128},{8,136},{16,144},{24,152},{32,160},{40,168},{48,176},{56,1... | collective-permute-start | bytes 258056 | tf_op jit(solution)/shard_map/ppermute | solution.py:44
  21.8 121.3 %reduce-scatter.2.cloned.1.call-start = ((), (), s32[]{:S(2)}) async-start(), calls=%async_computation.1 | async-start | bytes 3096576 | tf_op jit(solution)/shard_map/reduce_scatter | solution.py:456
  21.9 4.8 %collective-permute-start.6 = (bf16[96,384]{1,0:T(8,128)(2,1)S(1)}, bf16[96,384]{1,0:T(8,128)(2,1)S(1)}, u32[]{:S(2)}, u32[]{:S(2)}) collective-permute-start(bf16[96,384]{1,0:T(8,128)(2,1)S(1)} %get-tuple-element.58), channel_id=1, source_target_pairs={{0,128},{8,136},{16,144},{24,152},{32,160},{40,168},{48,176},{56,1... | collective-permute-start | bytes 221192 | tf_op jit(solution)/shard_map/ppermute | solution.py:44
  32.2 5.3 %collective-permute-start.10 = (bf16[2,96,384]{2,1,0:T(8,128)(2,1)S(1)}, bf16[2,96,384]{2,1,0:T(8,128)(2,1)S(1)}, u32[]{:S(2)}, u32[]{:S(2)}) collective-permute-start(bf16[2,96,384]{2,1,0:T(8,128)(2,1)S(1)} %get-tuple-element.57), channel_id=1, source_target_pairs={{0,6},{1,7},{2,4},{3,5},{4,2},{5,3},{6,0},{7,1},{8,14},{9,15},{10,... | collective-permute-start | bytes 442376 | tf_op jit(solution)/shard_map/ppermute | solution.py:65
  34.9 8.9 %collective-permute-start.9 = (bf16[2,2,96,384]{3,2,1,0:T(8,128)(2,1)S(1)}, bf16[2,2,96,384]{3,2,1,0:T(8,128)(2,1)S(1)}, u32[]{:S(2)}, u32[]{:S(2)}) collective-permute-start(bf16[2,2,96,384]{3,2,1,0:T(8,128)(2,1)S(1)} %pad_maximum_fusion.2), channel_id=1, source_target_pairs={{0,6},{1,7},{2,4},{3,5},{4,2},{5,3},{6,0},{7,1},{8,14},{9,15},{10,... | collective-permute-start | bytes 884744 | tf_op jit(solution)/shard_map/ppermute | solution.py:65
  37.6 6.4 %collective-permute-start.11 = (bf16[2,2,96,384]{3,2,1,0:T(8,128)(2,1)S(1)}, bf16[2,2,96,384]{3,2,1,0:T(8,128)(2,1)S(1)}, u32[]{:S(2)}, u32[]{:S(2)}) collective-permute-start(bf16[2,2,96,384]{3,2,1,0:T(8,128)(2,1)S(1)} %pad_maximum_fusion.3), channel_id=1, source_target_pairs={{0,2},{1,3},{2,0},{3,1},{4,6},{5,7},{6,4},{7,5},{8,10},{9,11},{10,... | collective-permute-start | bytes 884744 | tf_op jit(solution)/shard_map/ppermute | solution.py:65
  44.2 12.5 %collective-permute-start.12 = (bf16[2,4,2,96,384]{4,3,2,1,0:T(8,128)(2,1)S(1)}, bf16[2,4,2,96,384]{4,3,2,1,0:T(8,128)(2,1)S(1)}, u32[]{:S(2)}, u32[]{:S(2)}) collective-permute-start(bf16[2,4,2,96,384]{4,3,2,1,0:T(8,128)(2,1)S(1)} %pad_maximum_fusion.near_ref), channel_id=1, source_target_pairs={{0,8},{8,0},{16,24},{24,16},{32,40},{40,32},{48,56},{56,48},{64,72... | collective-permute-start | bytes 3538952 | tf_op jit(solution)/shard_map/ppermute | solution.py:44
  52.6 15.7 %collective-permute-start.1 = (bf16[96,672]{1,0:T(8,128)(2,1)}, bf16[96,672]{1,0:T(8,128)(2,1)S(1)}, u32[]{:S(2)}, u32[]{:S(2)}) collective-permute-start(bf16[96,672]{1,0:T(8,128)(2,1)} %get-tuple-element.27), channel_id=1, source_target_pairs={{0,8},{8,0},{16,24},{24,16},{32,40},{40,32},{48,56},{56,48},{64,72... | collective-permute-start | bytes 387080 | tf_op jit(solution)/shard_map/ppermute | solution.py:44
  53.2 15.1 %collective-permute-start.2 = (bf16[96,672]{1,0:T(8,128)(2,1)S(1)}, bf16[96,672]{1,0:T(8,128)(2,1)S(1)}, u32[]{:S(2)}, u32[]{:S(2)}) collective-permute-start(bf16[96,672]{1,0:T(8,128)(2,1)S(1)} %get-tuple-element.28), channel_id=1, source_target_pairs={{0,128},{8,136},{16,144},{24,152},{32,160},{40,168},{48,176},{56,1... | collective-permute-start | bytes 387080 | tf_op jit(solution)/shard_map/ppermute | solution.py:44
  55.3 13.0 %collective-permute-start.3 = (bf16[96,672]{1,0:T(8,128)(2,1)S(1)}, bf16[96,672]{1,0:T(8,128)(2,1)S(1)}, u32[]{:S(2)}, u32[]{:S(2)}) collective-permute-start(bf16[96,672]{1,0:T(8,128)(2,1)S(1)} %get-tuple-element.29), channel_id=1, source_target_pairs={{0,136},{8,128},{16,152},{24,144},{32,168},{40,160},{48,184},{56,1... | collective-permute-start | bytes 387080 | tf_op jit(solution)/shard_map/ppermute | solution.py:44
  101.2 5.9 %collective-permute-start.16 = (bf16[2,4,2,96,384]{4,3,2,1,0:T(8,128)(2,1)}, bf16[2,4,2,96,384]{4,3,2,1,0:T(8,128)(2,1)S(1)}, u32[]{:S(2)}, u32[]{:S(2)}) collective-permute-start(bf16[2,4,2,96,384]{4,3,2,1,0:T(8,128)(2,1)} %copy-done.11), channel_id=1, source_target_pairs={{0,8},{8,0},{16,24},{24,16},{32,40},{40,32},{48,56},{56,48},{64,72... | collective-permute-start | bytes 3538952 | tf_op jit(solution)/shard_map/ppermute | solution.py:44
  107.5 8.3 %collective-permute-start.19 = (bf16[2,2,96,384]{3,2,1,0:T(8,128)(2,1)S(1)}, bf16[2,2,96,384]{3,2,1,0:T(8,128)(2,1)S(1)}, u32[]{:S(2)}, u32[]{:S(2)}) collective-permute-start(bf16[2,2,96,384]{3,2,1,0:T(8,128)(2,1)S(1)} %get-tuple-element.48), channel_id=1, source_target_pairs={{0,2},{1,3},{2,0},{3,1},{4,6},{5,7},{6,4},{7,5},{8,10},{9,11},{10,... | collective-permute-start | bytes 884744 | tf_op jit(solution)/shard_map/ppermute | solution.py:65
  108.9 9.2 %collective-permute-start.17 = (bf16[2,2,96,384]{3,2,1,0:T(8,128)(2,1)S(1)}, bf16[2,2,96,384]{3,2,1,0:T(8,128)(2,1)S(1)}, u32[]{:S(2)}, u32[]{:S(2)}) collective-permute-start(bf16[2,2,96,384]{3,2,1,0:T(8,128)(2,1)S(1)} %get-tuple-element.49), channel_id=1, source_target_pairs={{0,6},{1,7},{2,4},{3,5},{4,2},{5,3},{6,0},{7,1},{8,14},{9,15},{10,... | collective-permute-start | bytes 884744 | tf_op jit(solution)/shard_map/ppermute | solution.py:65
  118.3 4.5 %collective-permute-start.18 = (bf16[2,96,384]{2,1,0:T(8,128)(2,1)S(1)}, bf16[2,96,384]{2,1,0:T(8,128)(2,1)S(1)}, u32[]{:S(2)}, u32[]{:S(2)}) collective-permute-start(bf16[2,96,384]{2,1,0:T(8,128)(2,1)S(1)} %fusion.9), channel_id=1, source_target_pairs={{0,2},{1,3},{2,0},{3,1},{4,6},{5,7},{6,4},{7,5},{8,10},{9,11},{10,... | collective-permute-start | bytes 442376 | tf_op jit(solution)/shard_map/ppermute | solution.py:65
  118.4 5.7 %collective-permute-start.20 = (bf16[2,96,384]{2,1,0:T(8,128)(2,1)S(1)}, bf16[2,96,384]{2,1,0:T(8,128)(2,1)S(1)}, u32[]{:S(2)}, u32[]{:S(2)}) collective-permute-start(bf16[2,96,384]{2,1,0:T(8,128)(2,1)S(1)} %fusion.10), channel_id=1, source_target_pairs={{0,6},{1,7},{2,4},{3,5},{4,2},{5,3},{6,0},{7,1},{8,14},{9,15},{10,... | collective-permute-start | bytes 442376 | tf_op jit(solution)/shard_map/ppermute | solution.py:65
  128.7 13.7 %collective-permute-start.22 = (bf16[96,384]{1,0:T(8,128)(2,1)S(1)}, bf16[96,384]{1,0:T(8,128)(2,1)S(1)}, u32[]{:S(2)}, u32[]{:S(2)}) collective-permute-start(bf16[96,384]{1,0:T(8,128)(2,1)S(1)} %get-tuple-element.51), channel_id=1, source_target_pairs={{0,128},{8,136},{16,144},{24,152},{32,160},{40,168},{48,176},{56,1... | collective-permute-start | bytes 221192 | tf_op jit(solution)/shard_map/ppermute | solution.py:44
  131.4 6.3 %collective-permute-start.13 = (bf16[96,224]{1,0:T(8,128)(2,1)S(1)}, bf16[96,224]{1,0:T(8,128)(2,1)S(1)}, u32[]{:S(2)}, u32[]{:S(2)}) collective-permute-start(bf16[96,224]{1,0:T(8,128)(2,1)S(1)} %get-tuple-element.34), channel_id=1, source_target_pairs={{0,8},{8,0},{16,24},{24,16},{32,40},{40,32},{48,56},{56,48},{64,72... | collective-permute-start | bytes 129032 | tf_op jit(solution)/shard_map/ppermute | solution.py:44
  134.6 4.9 %collective-permute-start.14 = (bf16[96,224]{1,0:T(8,128)(2,1)S(1)}, bf16[96,224]{1,0:T(8,128)(2,1)S(1)}, u32[]{:S(2)}, u32[]{:S(2)}) collective-permute-start(bf16[96,224]{1,0:T(8,128)(2,1)S(1)} %get-tuple-element.35), channel_id=1, source_target_pairs={{0,128},{8,136},{16,144},{24,152},{32,160},{40,168},{48,176},{56,1... | collective-permute-start | bytes 129032 | tf_op jit(solution)/shard_map/ppermute | solution.py:44
  134.9 5.7 %collective-permute-start.15 = (bf16[96,224]{1,0:T(8,128)(2,1)S(1)}, bf16[96,224]{1,0:T(8,128)(2,1)S(1)}, u32[]{:S(2)}, u32[]{:S(2)}) collective-permute-start(bf16[96,224]{1,0:T(8,128)(2,1)S(1)} %get-tuple-element.36), channel_id=1, source_target_pairs={{0,136},{8,128},{16,152},{24,144},{32,168},{40,160},{48,184},{56,1... | collective-permute-start | bytes 129032 | tf_op jit(solution)/shard_map/ppermute | solution.py:44
  145.9 7.8 %collective-permute-start.23 = (bf16[96,448]{1,0:T(8,128)(2,1)S(1)}, bf16[96,448]{1,0:T(8,128)(2,1)S(1)}, u32[]{:S(2)}, u32[]{:S(2)}) collective-permute-start(bf16[96,448]{1,0:T(8,128)(2,1)S(1)} %get-tuple-element.41), channel_id=1, source_target_pairs={{0,8},{8,0},{16,24},{24,16},{32,40},{40,32},{48,56},{56,48},{64,72... | collective-permute-start | bytes 258056 | tf_op jit(solution)/shard_map/ppermute | solution.py:44
  150.5 5.9 %collective-permute-start.24 = (bf16[96,448]{1,0:T(8,128)(2,1)S(1)}, bf16[96,448]{1,0:T(8,128)(2,1)S(1)}, u32[]{:S(2)}, u32[]{:S(2)}) collective-permute-start(bf16[96,448]{1,0:T(8,128)(2,1)S(1)} %get-tuple-element.42), channel_id=1, source_target_pairs={{0,128},{8,136},{16,144},{24,152},{32,160},{40,168},{48,176},{56,1... | collective-permute-start | bytes 258056 | tf_op jit(solution)/shard_map/ppermute | solution.py:44
  153.0 6.3 %collective-permute-start.25 = (bf16[96,448]{1,0:T(8,128)(2,1)S(1)}, bf16[96,448]{1,0:T(8,128)(2,1)S(1)}, u32[]{:S(2)}, u32[]{:S(2)}) collective-permute-start(bf16[96,448]{1,0:T(8,128)(2,1)S(1)} %get-tuple-element.43), channel_id=1, source_target_pairs={{0,136},{8,128},{16,152},{24,144},{32,168},{40,160},{48,184},{56,1... | collective-permute-start | bytes 258056 | tf_op jit(solution)/shard_map/ppermute | solution.py:44
  (18 other events, 95.7 us)
Sparse Core Ops, SparseCore 0:
  21.9 42.8 all-gather.2
  101.3 41.7 reduce-scatter.1

commit v4 on v3

--- a/solution.py
+++ b/solution.py
@@ -445,12 +445,12 @@
     bias_far = row_move(bias_near, 0, 0, 1)
     b2 = pl.pallas_call(
         functools.partial(bias_kernel, rows, keys),
-        in_specs=[SMEM] + [VMEM] * 4 + [HBM],
+        in_specs=[SMEM] + [VMEM] * 4 + [ANY],
         out_specs=VMEM,
         out_shape=jax.ShapeDtypeStruct((4 * rows, 32 * rows), F32),
         compiler_params=SMALL,
         name="bias",
-    )(pos, reach, chain_id.reshape(1, -1), bias_near, bias_far, kv)
+    )(pos, reach, chain_id.reshape(1, -1), bias_near, bias_far, kv[0, :16, :128])
 
     *dq, dkv, db_own, db_other = attn(pos, rows, keys, rest, kv, b2)
     summed = lax.psum_scatter(
@@ -460,7 +460,8 @@
         axis_index_groups=groups,
         tiled=True,
     )
-    (grad_q,) = join(pos, width, swap(dq), 1)
+    dq_parts = swap(dq)
+    (grad_q,) = join(pos, width, dq_parts, 1)
 
     db_sum = (db_own + row_move(db_other, 0, 0, 1).astype(F32)).astype(BF)
     total = []
@@ -474,7 +475,7 @@
     grad_bias = jnp.where(
         y == 0, jnp.stack([total[0], got]), jnp.stack([got, total[0]])
     )
-    back = swap(turn_out(pos, summed, grad_q, grad_bias))
+    back = swap(turn_out(pos, summed, *dq_parts[1:], grad_bias))
     grad_k, grad_v = join(pos, width, back, 2)
     return grad_q, grad_k, grad_v, grad_bias
 

time: 168 us -> 168 us (level)
  local copies, waits for them, and re-layouts: 7.2 us -> 5.16 us
    unnamed x28 -> x24, local copies, waits for them, and re-layouts: 6.6 us -> 3.9 us
    reduce_scatter x1, waiting for transfers between devices: 0.67 us -> 3.05 us  [per_device(): lax.psum_scatter(dkv.reshape(NZ * 2 * HALF * DH, 4 * rows), 'row', scatte...]
  transfers between devices with their start and end apart: 28 -> 28, of which waited for: 17 -> 17; matrix products, arithmetic and copies ran while one was open for 1% -> 2% of each run, Pallas kernels for 3% -> 3%
where the time goes in v4:
time: 168 us
  starting transfers between devices  51.7 us (31%)
  waiting for transfers between devices  51.3 us (31%)
  Pallas kernels  43.9 us (26%)
  between operations  14.5 us (9%)
  local copies, waits for them, and re-layouts  5.16 us (3%)
    ppermute x16, starting transfers between devices, row_move(): return lax.ppermute(array, 'row', pairs)  39 us
    pallas_call x1, Pallas kernels, attn(): pl.pallas_call(functools.partial(attn_kernel, rows, keys), in_specs=[SMEM...  32.9 us
    ppermute x8, waiting for transfers between devices, x_pair(): return lax.ppermute(array, 'col', pairs)  18.2 us
    ppermute x16, waiting for transfers between devices, row_move(): return lax.ppermute(array, 'row', pairs)  15.3 us
    ppermute x8, starting transfers between devices, x_pair(): return lax.ppermute(array, 'col', pairs)  10.8 us
    all_gather x1, waiting for transfers between devices, per_device(): kv = lax.all_gather(turn_in(pos, kv_parts), 'row', axis_index_groups=groups)  7.95 us
    ppermute x2, waiting for transfers between devices, col_move(): return lax.ppermute(array, 'col', pairs)  6.73 us
    unnamed x24, local copies, waits for them, and re-layouts  3.9 us
  transfers between devices with their start and end apart: 28, of which 17 were waited for; matrix products, arithmetic and copies ran while one was open for 2% of the time, Pallas kernels for 3%

profile of v4, /device:TPU:1, one launch (start us, length us, event | category | flops | bytes accessed | tf_op | source)
XLA Modules:
  0.0 167.8 jit_solution(10821677795260634158)
XLA Ops:
  9.6 4.4 %collective-permute-start = (bf16[96,448]{1,0:T(8,128)(2,1)S(1)}, bf16[96,448]{1,0:T(8,128)(2,1)S(1)}, u32[]{:S(2)}, u32[]{:S(2)}) collective-permute-start(bf16[96,448]{1,0:T(8,128)(2,1)S(1)} %get-tuple-element.25), channel_id=1, source_target_pairs={{0,136},{8,128},{16,152},{24,144},{32,168},{40,160},{48,184},{56,1... | collective-permute-start | bytes 258056 | tf_op jit(solution)/shard_map/ppermute | solution.py:44
  16.6 3.4 %collective-permute-done.5.refs_2_ = bf16[96,448]{1,0:T(8,128)(2,1)S(1)} collective-permute-done((bf16[96,448]{1,0:T(8,128)(2,1)S(1)}, bf16[96,448]{1,0:T(8,128)(2,1)S(1)}, u32[]{:S(2)}, u32[]{:S(2)}) %collective-permute-start.5) | collective-permute-done | bytes 86048 | tf_op jit(solution)/shard_map/ppermute | solution.py:44
  21.9 2.5 %collective-permute-start.6 = (bf16[96,384]{1,0:T(8,128)(2,1)S(1)}, bf16[96,384]{1,0:T(8,128)(2,1)S(1)}, u32[]{:S(2)}, u32[]{:S(2)}) collective-permute-start(bf16[96,384]{1,0:T(8,128)(2,1)S(1)} %get-tuple-element.58), channel_id=1, source_target_pairs={{0,128},{8,136},{16,144},{24,152},{32,160},{40,168},{48,176},{56,1... | collective-permute-start | bytes 221192 | tf_op jit(solution)/shard_map/ppermute | solution.py:44
  24.3 2.3 %collective-permute-done.6 = bf16[96,384]{1,0:T(8,128)(2,1)S(1)} collective-permute-done((bf16[96,384]{1,0:T(8,128)(2,1)S(1)}, bf16[96,384]{1,0:T(8,128)(2,1)S(1)}, u32[]{:S(2)}, u32[]{:S(2)}) %collective-permute-start.6) | collective-permute-done | bytes 73760 | tf_op jit(solution)/shard_map/ppermute | solution.py:44
  27.3 3.5 %collective-permute-done.7 = bf16[2,96,384]{2,1,0:T(8,128)(2,1)S(1)} collective-permute-done((bf16[2,96,384]{2,1,0:T(8,128)(2,1)S(1)}, bf16[2,96,384]{2,1,0:T(8,128)(2,1)S(1)}, u32[]{:S(2)}, u32[]{:S(2)}) %collective-permute-start.7) | collective-permute-done | bytes 147488 | tf_op jit(solution)/shard_map/ppermute | solution.py:52
  35.0 2.6 %collective-permute-start.9 = (bf16[2,2,96,384]{3,2,1,0:T(8,128)(2,1)S(1)}, bf16[2,2,96,384]{3,2,1,0:T(8,128)(2,1)S(1)}, u32[]{:S(2)}, u32[]{:S(2)}) collective-permute-start(bf16[2,2,96,384]{3,2,1,0:T(8,128)(2,1)S(1)} %pad_maximum_fusion.2), channel_id=1, source_target_pairs={{0,6},{1,7},{2,4},{3,5},{4,2},{5,3},{6,0},{7,1},{8,14},{9,15},{10,... | collective-permute-start | bytes 884744 | tf_op jit(solution)/shard_map/ppermute | solution.py:65
  37.7 6.2 %collective-permute-done.9 = bf16[2,2,96,384]{3,2,1,0:T(8,128)(2,1)S(1)} collective-permute-done((bf16[2,2,96,384]{3,2,1,0:T(8,128)(2,1)S(1)}, bf16[2,2,96,384]{3,2,1,0:T(8,128)(2,1)S(1)}, u32[]{:S(2)}, u32[]{:S(2)}) %collective-permute-start.9) | collective-permute-done | bytes 294944 | tf_op jit(solution)/shard_map/ppermute | solution.py:65
  44.3 6.4 %collective-permute-start.12 = (bf16[2,4,2,96,384]{4,3,2,1,0:T(8,128)(2,1)S(1)}, bf16[2,4,2,96,384]{4,3,2,1,0:T(8,128)(2,1)S(1)}, u32[]{:S(2)}, u32[]{:S(2)}) collective-permute-start(bf16[2,4,2,96,384]{4,3,2,1,0:T(8,128)(2,1)S(1)} %pad_maximum_fusion.near_ref), channel_id=1, source_target_pairs={{0,8},{8,0},{16,24},{24,16},{32,40},{40,32},{48,56},{56,48},{64,72... | collective-permute-start | bytes 3538952 | tf_op jit(solution)/shard_map/ppermute | solution.py:44
  53.5 2.1 %collective-permute-start.2 = (bf16[96,672]{1,0:T(8,128)(2,1)S(1)}, bf16[96,672]{1,0:T(8,128)(2,1)S(1)}, u32[]{:S(2)}, u32[]{:S(2)}) collective-permute-start(bf16[96,672]{1,0:T(8,128)(2,1)S(1)} %get-tuple-element.28), channel_id=1, source_target_pairs={{0,128},{8,136},{16,144},{24,152},{32,160},{40,168},{48,176},{56,1... | collective-permute-start | bytes 387080 | tf_op jit(solution)/shard_map/ppermute | solution.py:44
  56.7 7.9 %all-gather.3.cloned.1.call-done = bf16[3584,384]{1,0:T(8,128)(2,1)} async-done(((bf16[448,384]{1,0:T(8,128)(2,1)}), bf16[3584,384]{1,0:T(8,128)(2,1)}) %all-gather.3.cloned.1.call-update) | async-done | bytes 2752528 | tf_op jit(solution)/shard_map/all_gather | solution.py:423
  67.1 32.9 %attn.1 = (bf16[96,224]{1,0:T(8,128)(2,1)S(1)}, bf16[96,224]{1,0:T(8,128)(2,1)S(1)}, bf16[96,224]{1,0:T(8,128)(2,1)S(1)}, bf16[96,224]{1,0:T(8,128)(2,1)S(1)}, b...) custom-call(s32[5]{0:T(128)S(1)} %stack.87.pos_ref.me_ref, ...), custom_call_target="tpu_custom_call" | custom-call | flops 62999998464 | bytes 11796480 | tf_op jit(solution)/shard_map/attn/pallas_call | solution.py:388
  101.1 3.3 %collective-permute-start.16 = (bf16[2,4,2,96,384]{4,3,2,1,0:T(8,128)(2,1)}, bf16[2,4,2,96,384]{4,3,2,1,0:T(8,128)(2,1)S(1)}, u32[]{:S(2)}, u32[]{:S(2)}) collective-permute-start(bf16[2,4,2,96,384]{4,3,2,1,0:T(8,128)(2,1)} %copy-done.9), channel_id=1, source_target_pairs={{0,8},{8,0},{16,24},{24,16},{32,40},{40,32},{48,56},{56,48},{64,72... | collective-permute-start | bytes 3538952 | tf_op jit(solution)/shard_map/ppermute | solution.py:44
  104.4 2.7 %collective-permute-done.16 = bf16[2,4,2,96,384]{4,3,2,1,0:T(8,128)(2,1)S(1)} collective-permute-done((bf16[2,4,2,96,384]{4,3,2,1,0:T(8,128)(2,1)}, bf16[2,4,2,96,384]{4,3,2,1,0:T(8,128)(2,1)S(1)}, u32[]{:S(2)}, u32[]{:S(2)}) %collective-permute-start.16) | collective-permute-done | bytes 1179680 | tf_op jit(solution)/shard_map/ppermute | solution.py:44
  110.5 5.2 %collective-permute-done.19 = bf16[2,2,96,384]{3,2,1,0:T(8,128)(2,1)S(1)} collective-permute-done((bf16[2,2,96,384]{3,2,1,0:T(8,128)(2,1)S(1)}, bf16[2,2,96,384]{3,2,1,0:T(8,128)(2,1)S(1)}, u32[]{:S(2)}, u32[]{:S(2)}) %collective-permute-start.19) | collective-permute-done | bytes 294944 | tf_op jit(solution)/shard_map/ppermute | solution.py:65
  115.8 2.1 %collective-permute-done.17 = bf16[2,2,96,384]{3,2,1,0:T(8,128)(2,1)S(1)} collective-permute-done((bf16[2,2,96,384]{3,2,1,0:T(8,128)(2,1)S(1)}, bf16[2,2,96,384]{3,2,1,0:T(8,128)(2,1)S(1)}, u32[]{:S(2)}, u32[]{:S(2)}) %collective-permute-start.17) | collective-permute-done | bytes 294944 | tf_op jit(solution)/shard_map/ppermute | solution.py:65
  120.0 2.6 %collective-permute-done.18 = bf16[2,96,384]{2,1,0:T(8,128)(2,1)S(1)} collective-permute-done((bf16[2,96,384]{2,1,0:T(8,128)(2,1)S(1)}, bf16[2,96,384]{2,1,0:T(8,128)(2,1)S(1)}, u32[]{:S(2)}, u32[]{:S(2)}) %collective-permute-start.18) | collective-permute-done | bytes 147488 | tf_op jit(solution)/shard_map/ppermute | solution.py:65
  125.1 3.2 %collective-permute-done.21 = bf16[2,96,384]{2,1,0:T(8,128)(2,1)S(1)} collective-permute-done((bf16[2,96,384]{2,1,0:T(8,128)(2,1)S(1)}, bf16[2,96,384]{2,1,0:T(8,128)(2,1)S(1)}, u32[]{:S(2)}, u32[]{:S(2)}) %collective-permute-start.21) | collective-permute-done | bytes 147488 | tf_op jit(solution)/shard_map/ppermute | solution.py:52
  128.4 2.8 %collective-permute-start.22 = (bf16[96,384]{1,0:T(8,128)(2,1)S(1)}, bf16[96,384]{1,0:T(8,128)(2,1)S(1)}, u32[]{:S(2)}, u32[]{:S(2)}) collective-permute-start(bf16[96,384]{1,0:T(8,128)(2,1)S(1)} %get-tuple-element.51), channel_id=1, source_target_pairs={{0,128},{8,136},{16,144},{24,152},{32,160},{40,168},{48,176},{56,1... | collective-permute-start | bytes 221192 | tf_op jit(solution)/shard_map/ppermute | solution.py:44
  131.2 3.4 %collective-permute-start.13 = (bf16[96,224]{1,0:T(8,128)(2,1)S(1)}, bf16[96,224]{1,0:T(8,128)(2,1)S(1)}, u32[]{:S(2)}, u32[]{:S(2)}) collective-permute-start(bf16[96,224]{1,0:T(8,128)(2,1)S(1)} %get-tuple-element.34), channel_id=1, source_target_pairs={{0,8},{8,0},{16,24},{24,16},{32,40},{40,32},{48,56},{56,48},{64,72... | collective-permute-start | bytes 129032 | tf_op jit(solution)/shard_map/ppermute | solution.py:44
  134.9 2.8 %collective-permute-start.15 = (bf16[96,224]{1,0:T(8,128)(2,1)S(1)}, bf16[96,224]{1,0:T(8,128)(2,1)S(1)}, u32[]{:S(2)}, u32[]{:S(2)}) collective-permute-start(bf16[96,224]{1,0:T(8,128)(2,1)S(1)} %get-tuple-element.36), channel_id=1, source_target_pairs={{0,136},{8,128},{16,152},{24,144},{32,168},{40,160},{48,184},{56,1... | collective-permute-start | bytes 129032 | tf_op jit(solution)/shard_map/ppermute | solution.py:44
  140.6 3.0 %reduce-scatter.2.cloned.1.call-done.in_ref = bf16[448,384]{1,0:T(8,128)(2,1)} async-done(((bf16[3584,384]{1,0:T(8,128)(2,1)}), bf16[448,384]{1,0:T(8,128)(2,1)}) %reduce-scatter.2.cloned.1.call-update) | async-done | bytes 344080 | tf_op jit(solution)/shard_map/reduce_scatter | solution.py:456
  145.6 4.4 %collective-permute-start.23 = (bf16[96,448]{1,0:T(8,128)(2,1)S(1)}, bf16[96,448]{1,0:T(8,128)(2,1)S(1)}, u32[]{:S(2)}, u32[]{:S(2)}) collective-permute-start(bf16[96,448]{1,0:T(8,128)(2,1)S(1)} %get-tuple-element.41), channel_id=1, source_target_pairs={{0,8},{8,0},{16,24},{24,16},{32,40},{40,32},{48,56},{56,48},{64,72... | collective-permute-start | bytes 258056 | tf_op jit(solution)/shard_map/ppermute | solution.py:44
  150.0 2.7 %collective-permute-start.24 = (bf16[96,448]{1,0:T(8,128)(2,1)S(1)}, bf16[96,448]{1,0:T(8,128)(2,1)S(1)}, u32[]{:S(2)}, u32[]{:S(2)}) collective-permute-start(bf16[96,448]{1,0:T(8,128)(2,1)S(1)} %get-tuple-element.42), channel_id=1, source_target_pairs={{0,128},{8,136},{16,144},{24,152},{32,160},{40,168},{48,176},{56,1... | collective-permute-start | bytes 258056 | tf_op jit(solution)/shard_map/ppermute | solution.py:44
  155.8 3.1 %collective-permute-done.25.refs_3_ = bf16[96,448]{1,0:T(8,128)(2,1)S(1)} collective-permute-done((bf16[96,448]{1,0:T(8,128)(2,1)S(1)}, bf16[96,448]{1,0:T(8,128)(2,1)S(1)}, u32[]{:S(2)}, u32[]{:S(2)}) %collective-permute-start.25) | collective-permute-done | bytes 86048 | tf_op jit(solution)/shard_map/ppermute | solution.py:44
  (96 shorter events, 37.8 us)
Async XLA Ops:
  7.2 57.5 %all-gather.3.cloned.1.call-start = ((), (), s32[]{:S(2)}) async-start(), calls=%async_computation.2 | async-start | bytes 3096576 | tf_op jit(solution)/shard_map/all_gather | solution.py:423
  9.6 7.0 %collective-permute-start = (bf16[96,448]{1,0:T(8,128)(2,1)S(1)}, bf16[96,448]{1,0:T(8,128)(2,1)S(1)}, u32[]{:S(2)}, u32[]{:S(2)}) collective-permute-start(bf16[96,448]{1,0:T(8,128)(2,1)S(1)} %get-tuple-element.25), channel_id=1, source_target_pairs={{0,136},{8,128},{16,152},{24,144},{32,168},{40,160},{48,184},{56,1... | collective-permute-start | bytes 258056 | tf_op jit(solution)/shard_map/ppermute | solution.py:44
  14.0 6.0 %collective-permute-start.5 = (bf16[96,448]{1,0:T(8,128)(2,1)S(1)}, bf16[96,448]{1,0:T(8,128)(2,1)S(1)}, u32[]{:S(2)}, u32[]{:S(2)}) collective-permute-start(bf16[96,448]{1,0:T(8,128)(2,1)S(1)} %get-tuple-element.30.refs_2_), channel_id=1, source_target_pairs={{0,128},{8,136},{16,144},{24,152},{32,160},{40,168},{48,176},{56,1... | collective-permute-start | bytes 258056 | tf_op jit(solution)/shard_map/ppermute | solution.py:44
  21.8 121.9 %reduce-scatter.2.cloned.1.call-start = ((), (), s32[]{:S(2)}) async-start(), calls=%async_computation.1 | async-start | bytes 3096576 | tf_op jit(solution)/shard_map/reduce_scatter | solution.py:456
  21.9 4.8 %collective-permute-start.6 = (bf16[96,384]{1,0:T(8,128)(2,1)S(1)}, bf16[96,384]{1,0:T(8,128)(2,1)S(1)}, u32[]{:S(2)}, u32[]{:S(2)}) collective-permute-start(bf16[96,384]{1,0:T(8,128)(2,1)S(1)} %get-tuple-element.58), channel_id=1, source_target_pairs={{0,128},{8,136},{16,144},{24,152},{32,160},{40,168},{48,176},{56,1... | collective-permute-start | bytes 221192 | tf_op jit(solution)/shard_map/ppermute | solution.py:44
  32.2 5.3 %collective-permute-start.10 = (bf16[2,96,384]{2,1,0:T(8,128)(2,1)S(1)}, bf16[2,96,384]{2,1,0:T(8,128)(2,1)S(1)}, u32[]{:S(2)}, u32[]{:S(2)}) collective-permute-start(bf16[2,96,384]{2,1,0:T(8,128)(2,1)S(1)} %get-tuple-element.57), channel_id=1, source_target_pairs={{0,6},{1,7},{2,4},{3,5},{4,2},{5,3},{6,0},{7,1},{8,14},{9,15},{10,... | collective-permute-start | bytes 442376 | tf_op jit(solution)/shard_map/ppermute | solution.py:65
  35.0 8.9 %collective-permute-start.9 = (bf16[2,2,96,384]{3,2,1,0:T(8,128)(2,1)S(1)}, bf16[2,2,96,384]{3,2,1,0:T(8,128)(2,1)S(1)}, u32[]{:S(2)}, u32[]{:S(2)}) collective-permute-start(bf16[2,2,96,384]{3,2,1,0:T(8,128)(2,1)S(1)} %pad_maximum_fusion.2), channel_id=1, source_target_pairs={{0,6},{1,7},{2,4},{3,5},{4,2},{5,3},{6,0},{7,1},{8,14},{9,15},{10,... | collective-permute-start | bytes 884744 | tf_op jit(solution)/shard_map/ppermute | solution.py:65
  37.6 6.4 %collective-permute-start.11 = (bf16[2,2,96,384]{3,2,1,0:T(8,128)(2,1)S(1)}, bf16[2,2,96,384]{3,2,1,0:T(8,128)(2,1)S(1)}, u32[]{:S(2)}, u32[]{:S(2)}) collective-permute-start(bf16[2,2,96,384]{3,2,1,0:T(8,128)(2,1)S(1)} %pad_maximum_fusion.3), channel_id=1, source_target_pairs={{0,2},{1,3},{2,0},{3,1},{4,6},{5,7},{6,4},{7,5},{8,10},{9,11},{10,... | collective-permute-start | bytes 884744 | tf_op jit(solution)/shard_map/ppermute | solution.py:65
  44.3 21.1 %collective-permute-start.12 = (bf16[2,4,2,96,384]{4,3,2,1,0:T(8,128)(2,1)S(1)}, bf16[2,4,2,96,384]{4,3,2,1,0:T(8,128)(2,1)S(1)}, u32[]{:S(2)}, u32[]{:S(2)}) collective-permute-start(bf16[2,4,2,96,384]{4,3,2,1,0:T(8,128)(2,1)S(1)} %pad_maximum_fusion.near_ref), channel_id=1, source_target_pairs={{0,8},{8,0},{16,24},{24,16},{32,40},{40,32},{48,56},{56,48},{64,72... | collective-permute-start | bytes 3538952 | tf_op jit(solution)/shard_map/ppermute | solution.py:44
  53.1 14.0 %collective-permute-start.1 = (bf16[96,672]{1,0:T(8,128)(2,1)}, bf16[96,672]{1,0:T(8,128)(2,1)S(1)}, u32[]{:S(2)}, u32[]{:S(2)}) collective-permute-start(bf16[96,672]{1,0:T(8,128)(2,1)} %get-tuple-element.27), channel_id=1, source_target_pairs={{0,8},{8,0},{16,24},{24,16},{32,40},{40,32},{48,56},{56,48},{64,72... | collective-permute-start | bytes 387080 | tf_op jit(solution)/shard_map/ppermute | solution.py:44
  53.5 13.6 %collective-permute-start.2 = (bf16[96,672]{1,0:T(8,128)(2,1)S(1)}, bf16[96,672]{1,0:T(8,128)(2,1)S(1)}, u32[]{:S(2)}, u32[]{:S(2)}) collective-permute-start(bf16[96,672]{1,0:T(8,128)(2,1)S(1)} %get-tuple-element.28), channel_id=1, source_target_pairs={{0,128},{8,136},{16,144},{24,152},{32,160},{40,168},{48,176},{56,1... | collective-permute-start | bytes 387080 | tf_op jit(solution)/shard_map/ppermute | solution.py:44
  55.6 11.5 %collective-permute-start.3 = (bf16[96,672]{1,0:T(8,128)(2,1)S(1)}, bf16[96,672]{1,0:T(8,128)(2,1)S(1)}, u32[]{:S(2)}, u32[]{:S(2)}) collective-permute-start(bf16[96,672]{1,0:T(8,128)(2,1)S(1)} %get-tuple-element.29), channel_id=1, source_target_pairs={{0,136},{8,128},{16,152},{24,144},{32,168},{40,160},{48,184},{56,1... | collective-permute-start | bytes 387080 | tf_op jit(solution)/shard_map/ppermute | solution.py:44
  101.1 6.0 %collective-permute-start.16 = (bf16[2,4,2,96,384]{4,3,2,1,0:T(8,128)(2,1)}, bf16[2,4,2,96,384]{4,3,2,1,0:T(8,128)(2,1)S(1)}, u32[]{:S(2)}, u32[]{:S(2)}) collective-permute-start(bf16[2,4,2,96,384]{4,3,2,1,0:T(8,128)(2,1)} %copy-done.9), channel_id=1, source_target_pairs={{0,8},{8,0},{16,24},{24,16},{32,40},{40,32},{48,56},{56,48},{64,72... | collective-permute-start | bytes 3538952 | tf_op jit(solution)/shard_map/ppermute | solution.py:44
  107.5 8.3 %collective-permute-start.19 = (bf16[2,2,96,384]{3,2,1,0:T(8,128)(2,1)S(1)}, bf16[2,2,96,384]{3,2,1,0:T(8,128)(2,1)S(1)}, u32[]{:S(2)}, u32[]{:S(2)}) collective-permute-start(bf16[2,2,96,384]{3,2,1,0:T(8,128)(2,1)S(1)} %get-tuple-element.48), channel_id=1, source_target_pairs={{0,2},{1,3},{2,0},{3,1},{4,6},{5,7},{6,4},{7,5},{8,10},{9,11},{10,... | collective-permute-start | bytes 884744 | tf_op jit(solution)/shard_map/ppermute | solution.py:65
  108.8 9.1 %collective-permute-start.17 = (bf16[2,2,96,384]{3,2,1,0:T(8,128)(2,1)S(1)}, bf16[2,2,96,384]{3,2,1,0:T(8,128)(2,1)S(1)}, u32[]{:S(2)}, u32[]{:S(2)}) collective-permute-start(bf16[2,2,96,384]{3,2,1,0:T(8,128)(2,1)S(1)} %get-tuple-element.49), channel_id=1, source_target_pairs={{0,6},{1,7},{2,4},{3,5},{4,2},{5,3},{6,0},{7,1},{8,14},{9,15},{10,... | collective-permute-start | bytes 884744 | tf_op jit(solution)/shard_map/ppermute | solution.py:65
  118.1 4.5 %collective-permute-start.18 = (bf16[2,96,384]{2,1,0:T(8,128)(2,1)S(1)}, bf16[2,96,384]{2,1,0:T(8,128)(2,1)S(1)}, u32[]{:S(2)}, u32[]{:S(2)}) collective-permute-start(bf16[2,96,384]{2,1,0:T(8,128)(2,1)S(1)} %fusion.9), channel_id=1, source_target_pairs={{0,2},{1,3},{2,0},{3,1},{4,6},{5,7},{6,4},{7,5},{8,10},{9,11},{10,... | collective-permute-start | bytes 442376 | tf_op jit(solution)/shard_map/ppermute | solution.py:65
  118.2 5.6 %collective-permute-start.20 = (bf16[2,96,384]{2,1,0:T(8,128)(2,1)S(1)}, bf16[2,96,384]{2,1,0:T(8,128)(2,1)S(1)}, u32[]{:S(2)}, u32[]{:S(2)}) collective-permute-start(bf16[2,96,384]{2,1,0:T(8,128)(2,1)S(1)} %fusion.10), channel_id=1, source_target_pairs={{0,6},{1,7},{2,4},{3,5},{4,2},{5,3},{6,0},{7,1},{8,14},{9,15},{10,... | collective-permute-start | bytes 442376 | tf_op jit(solution)/shard_map/ppermute | solution.py:65
  128.4 9.3 %collective-permute-start.22 = (bf16[96,384]{1,0:T(8,128)(2,1)S(1)}, bf16[96,384]{1,0:T(8,128)(2,1)S(1)}, u32[]{:S(2)}, u32[]{:S(2)}) collective-permute-start(bf16[96,384]{1,0:T(8,128)(2,1)S(1)} %get-tuple-element.51), channel_id=1, source_target_pairs={{0,128},{8,136},{16,144},{24,152},{32,160},{40,168},{48,176},{56,1... | collective-permute-start | bytes 221192 | tf_op jit(solution)/shard_map/ppermute | solution.py:44
  131.2 6.5 %collective-permute-start.13 = (bf16[96,224]{1,0:T(8,128)(2,1)S(1)}, bf16[96,224]{1,0:T(8,128)(2,1)S(1)}, u32[]{:S(2)}, u32[]{:S(2)}) collective-permute-start(bf16[96,224]{1,0:T(8,128)(2,1)S(1)} %get-tuple-element.34), channel_id=1, source_target_pairs={{0,8},{8,0},{16,24},{24,16},{32,40},{40,32},{48,56},{56,48},{64,72... | collective-permute-start | bytes 129032 | tf_op jit(solution)/shard_map/ppermute | solution.py:44
  134.5 4.9 %collective-permute-start.14 = (bf16[96,224]{1,0:T(8,128)(2,1)S(1)}, bf16[96,224]{1,0:T(8,128)(2,1)S(1)}, u32[]{:S(2)}, u32[]{:S(2)}) collective-permute-start(bf16[96,224]{1,0:T(8,128)(2,1)S(1)} %get-tuple-element.35), channel_id=1, source_target_pairs={{0,128},{8,136},{16,144},{24,152},{32,160},{40,168},{48,176},{56,1... | collective-permute-start | bytes 129032 | tf_op jit(solution)/shard_map/ppermute | solution.py:44
  134.9 5.7 %collective-permute-start.15 = (bf16[96,224]{1,0:T(8,128)(2,1)S(1)}, bf16[96,224]{1,0:T(8,128)(2,1)S(1)}, u32[]{:S(2)}, u32[]{:S(2)}) collective-permute-start(bf16[96,224]{1,0:T(8,128)(2,1)S(1)} %get-tuple-element.36), channel_id=1, source_target_pairs={{0,136},{8,128},{16,152},{24,144},{32,168},{40,160},{48,184},{56,1... | collective-permute-start | bytes 129032 | tf_op jit(solution)/shard_map/ppermute | solution.py:44
  145.6 9.4 %collective-permute-start.23 = (bf16[96,448]{1,0:T(8,128)(2,1)S(1)}, bf16[96,448]{1,0:T(8,128)(2,1)S(1)}, u32[]{:S(2)}, u32[]{:S(2)}) collective-permute-start(bf16[96,448]{1,0:T(8,128)(2,1)S(1)} %get-tuple-element.41), channel_id=1, source_target_pairs={{0,8},{8,0},{16,24},{24,16},{32,40},{40,32},{48,56},{56,48},{64,72... | collective-permute-start | bytes 258056 | tf_op jit(solution)/shard_map/ppermute | solution.py:44
  150.0 5.9 %collective-permute-start.24 = (bf16[96,448]{1,0:T(8,128)(2,1)S(1)}, bf16[96,448]{1,0:T(8,128)(2,1)S(1)}, u32[]{:S(2)}, u32[]{:S(2)}) collective-permute-start(bf16[96,448]{1,0:T(8,128)(2,1)S(1)} %get-tuple-element.42), channel_id=1, source_target_pairs={{0,128},{8,136},{16,144},{24,152},{32,160},{40,168},{48,176},{56,1... | collective-permute-start | bytes 258056 | tf_op jit(solution)/shard_map/ppermute | solution.py:44
  152.6 6.3 %collective-permute-start.25 = (bf16[96,448]{1,0:T(8,128)(2,1)S(1)}, bf16[96,448]{1,0:T(8,128)(2,1)S(1)}, u32[]{:S(2)}, u32[]{:S(2)}) collective-permute-start(bf16[96,448]{1,0:T(8,128)(2,1)S(1)} %get-tuple-element.43), channel_id=1, source_target_pairs={{0,136},{8,128},{16,152},{24,144},{32,168},{40,160},{48,184},{56,1... | collective-permute-start | bytes 258056 | tf_op jit(solution)/shard_map/ppermute | solution.py:44
  (16 other events, 93.0 us)
Sparse Core Ops, SparseCore 0:
  21.9 42.7 all-gather.2
  101.2 42.3 reduce-scatter.1
